TPU v7x, 32 devices: a whole 2x2x4 slice. The times are simulated.
32 devices in a mesh: grp: 2 (over y), chan: 4 (over z), tblk: 4 (over x, core).
Axes of the slice: x: 2, y: 2, z: 4, core: 2. Of those that a mesh axis runs over, the one named last changes fastest.
Arguments:
- coarse_volts: bfloat16 [2048, 2, 2, 3072], P('chan', None, 'grp', 'tblk'), parts along dimension 2, may hold values from -6 to 6
- lead_in: bfloat16 [2048, 2, 2, 48], P('chan', None, 'grp'), parts along dimension 2, may hold values from -6 to 6
- slot_of_input: int32 [2048], replicated, may hold values from 0 to 2047, each once
Outputs:
- fine_voltages: bfloat16 [8, 192, 4096], P(('grp', 'chan'), 'tblk'), parts along dimension 0
- visibilities: bfloat16 [8, 4096, 4096], P(('grp', 'chan'), 'tblk'), parts along dimension 0
There are 2 independent parts, one for each index of `grp`. A program takes and returns all parts, laid end to end along the dimension named above; an argument that names none is the same for every part. Nothing has to cross between parts.
Inputs may be any that keep to these rules, and one draw needn't show every extreme that they name: `slot_of_input`: each slot holds exactly one input.
All inputs are finite; a program needn't handle non-finite values.
Results may differ from a plain program's by a relative error of at most 0.0057.
Values may be sent and summed in bfloat16 or wider, within the bound.
No kernel may reach another device: no remote copies, remote signals or barrier semaphores. Data moves between devices by JAX's collectives and lax.ppermute only.
A program may use at most 64 MiB of HBM per device.

v0:
```python
import math

import jax
import jax.numpy as jnp
from jax import lax
from jax.sharding import PartitionSpec as P

UPCHAN = 16
TAPS = 4
CH_DEV = 1


def shifted(value, axis, steps):
    count = lax.axis_size(axis)
    leading, last = (max(0, -steps), min(count, count - steps))
    return lax.ppermute(value, axis, [(source, source + steps) for source in range(leading, last)])


def filter_table():
    length = TAPS * UPCHAN
    taps = jnp.arange(length, dtype=jnp.int32)
    place = taps.astype(jnp.float32)
    center = (length - 1) / 2.0
    window = jnp.sinc((place - center) / UPCHAN) * (
        0.5 - 0.5 * jnp.cos(2.0 * math.pi * (place + 0.5) / length)
    )
    window = window / jnp.sqrt(jnp.sum(window * window))
    bins = jnp.arange(UPCHAN, dtype=jnp.int32)
    turns = (taps % UPCHAN)[:, None] * bins[None, :] % UPCHAN
    phase = 2.0 * math.pi * turns.astype(jnp.float32) / UPCHAN
    cosine = window[:, None] * jnp.cos(phase)
    sine = window[:, None] * jnp.sin(phase)
    from_real = jnp.stack([cosine, -sine], axis=1)
    from_imag = jnp.stack([sine, cosine], axis=1)
    table = jnp.stack([from_real, from_imag], axis=0)
    return table.reshape(2, TAPS, UPCHAN, 2, UPCHAN)


def channelize(volts, history):
    extended = jnp.concatenate([history, volts], axis=3).astype(jnp.float32)
    inputs, parts, coarse, length = extended.shape
    count = length // UPCHAN
    frames = count - TAPS + 1
    blocks = extended.reshape(inputs, parts, coarse, count, UPCHAN)
    table = filter_table()
    total = jnp.zeros((coarse, UPCHAN, frames, 2, inputs), jnp.float32)
    for step in range(TAPS):
        total = total + jnp.einsum(
            "ipctr,prok->cktoi",
            blocks[:, :, :, step : step + frames, :],
            table[:, step],
            precision=lax.Precision.HIGHEST,
        )
    return total.reshape(coarse * UPCHAN, frames, 2, inputs)


def local(coarse_volts, lead_in, slot_of_input):
    lead_width = lead_in.shape[3]
    tail = coarse_volts[:, :, :, coarse_volts.shape[3] - lead_width :]
    earlier = shifted(tail, "tblk", 1)
    block = lax.axis_index("tblk")
    blocks = lax.axis_size("tblk")
    history = jnp.where(block == 0, lead_in, earlier)
    window_channels = CH_DEV * lax.axis_size("chan")
    spectrum = channelize(coarse_volts, history)[:window_channels].astype(jnp.bfloat16)
    spectra_dev = spectrum.shape[1]
    all_time = lax.all_gather(spectrum, "tblk", axis=1, tiled=True)
    owned = lax.all_to_all(all_time, "chan", split_axis=0, concat_axis=3, tiled=True)
    ordered = jnp.take(owned, slot_of_input, axis=3)
    series = ordered.reshape(ordered.shape[0], ordered.shape[1], 2 * ordered.shape[3])
    width = series.shape[2]
    rows = width // blocks
    tile = lax.dynamic_slice_in_dim(series, block * rows, rows, 2)
    gram = jnp.einsum("ctr,ctk->crk", tile, series, preferred_element_type=jnp.float32)
    fine_out = lax.dynamic_slice_in_dim(series, block * spectra_dev, spectra_dev, 1)
    total_time = spectra_dev * blocks
    visibilities = (gram / total_time).astype(jnp.bfloat16)
    return (fine_out, visibilities)


def solution(mesh):
    placed = (P("chan", None, "grp", "tblk"), P("chan", None, "grp", None), P())
    return jax.shard_map(
        local,
        mesh=mesh,
        in_specs=placed,
        out_specs=(P(("grp", "chan"), "tblk", None), P(("grp", "chan"), "tblk", None)),
        check_vma=False,
    )
```

profile of v0, /device:TPU:0, one launch (start us, length us, event | category | flops | bytes accessed | tf_op | source)
XLA Modules:
  0.0 146.7 jit_solution(9041248661830303713)
XLA Ops:
  7.2 0.0 copy-start.2
  7.2 0.0 all-gather.3.cloned.1.call-start
  7.2 3.6 %copy.27 = bf16[512,2,1,768]{0,3,1,2:T(8,128)(2,1)S(1)} copy(bf16[512,2,1,768]{3,1,2,0:T(2,128)(2,1)} %param.3) | data formatting | bytes 3145728 | tf_op args[0]
  10.8 2.4 %collective-permute-start = (bf16[512,2,1,48]{0,3,1,2:T(8,128)(2,1)S(1)}, bf16[512,2,1,48]{0,3,1,2:T(8,128)(2,1)S(1)}, u32[]{:S(2)}, u32[]{:S(2)}) collective-permute-start(bf16[512,2,1,48]{0,3,1,2:T(8,128)(2,1)S(1)} %slice.45), channel_id=1, source_target_pairs={{0,1},{1,2},{2,3},{4,5},{5,6},{6,7},{8,9},{9,10},{10,11},{12,13},{... | collective-permute-start | bytes 294920 | tf_op jit(solution)/shard_map/ppermute | solution.py:16
  13.2 0.7 fusion.38
  14.6 0.1 fusion.22
  14.6 0.2 fusion.14
  14.8 0.0 collective-permute-done
  14.8 0.0 copy-done.2
  14.8 0.1 pad_maximum_fusion
  15.0 0.9 fusion.40
  15.8 1.5 %fusion.2 = f32[2,16,512,48,1]{2,1,4,3,0:T(8,128)S(1)} fusion(bf16[512,2,1,48,16]{0,4,3,1,2:T(8,128)(2,1)S(1)} %get-tuple-element.3, f32[2,4,16,2,16]{2,4,0,3,1:T(8,128)S(1)} %maximum_maximum_fusion), kind=kOutput, calls=%fused_computation.11 | convolution fusion | flops 301989888 | bytes 4751360 | tf_op jit(solution)/shard_map/ipctr,prok->cktoi/dot_general | solution.py:48
  17.4 1.5 %fusion.3 = f32[2,16,512,48,1]{2,1,4,3,0:T(8,128)S(1)} fusion(bf16[512,2,1,48,16]{0,4,3,1,2:T(8,128)(2,1)S(1)} %get-tuple-element.4, f32[2,4,16,2,16]{2,4,0,3,1:T(8,128)S(1)} %maximum_maximum_fusion), kind=kOutput, calls=%fused_computation.13 | convolution fusion | flops 301989888 | bytes 4751360 | tf_op jit(solution)/shard_map/ipctr,prok->cktoi/dot_general | solution.py:48
  18.9 1.5 %fusion.4 = f32[2,16,512,48,1]{2,1,4,3,0:T(8,128)S(1)} fusion(bf16[512,2,1,48,16]{0,4,3,1,2:T(8,128)(2,1)S(1)} %get-tuple-element.2, f32[2,4,16,2,16]{2,4,0,3,1:T(8,128)S(1)} %maximum_maximum_fusion), kind=kOutput, calls=%fused_computation.15 | convolution fusion | flops 301989888 | bytes 4751360 | tf_op jit(solution)/shard_map/ipctr,prok->cktoi/dot_general | solution.py:48
  20.4 1.9 %fusion.5 = bf16[1,16,48,2,512]{4,1,2,3,0:T(8,128)(2,1)S(1)} fusion(bf16[512,2,1,48,16]{0,4,3,1,2:T(8,128)(2,1)S(1)} %get-tuple-element.5, f32[2,16,512,48,1]{2,1,4,3,0:T(8,128)S(1)} %fusion.2, f32[2,16,512,48,1]{2,1,4,3,0:T(8,128)S(1)} %fusion.3, f32[2,16,512,48,1]{2,1,4,3,0:T(8,128)S(1)} %fusion.4, f32[2,4,16,2,16]{2,4,0,3,1:T(8,128)S(1)} %maximum_maximum_fusion), kind=kOutput, calls=%fused_computation.17 | convolution fusion | flops 305135616 | bytes 12615680 | tf_op jit(solution)/shard_map/ipctr,prok->cktoi/dot_general | solution.py:48
  22.3 0.9 slice.53
  23.2 0.0 all-gather.3.cloned.1.call-update
  23.2 24.5 %all-gather.3.cloned.1.call-done = bf16[1,4,192,2,512]{4,1,2,3,0:T(4,128)(2,1)} async-done(((bf16[1,4,48,2,512]{4,1,2,3,0:T(4,128)(2,1)}), bf16[1,4,192,2,512]{4,1,2,3,0:T(4,128)(2,1)}) %all-gather.3.cloned.1.call-update) | async-done | bytes 1572880 | tf_op jit(solution)/shard_map/all_gather | solution.py:67
  47.7 2.9 %copy.34 = bf16[4,192,2,512]{3,1,2,0:T(8,128)(2,1)} copy(bf16[4,192,2,512]{3,0,1,2:T(4,128)(2,1)} %bitcast.98) | data formatting | bytes 3145728 | tf_op jit(solution)/shard_map/all_gather | solution.py:67
  50.5 4.7 %all-to-all-start = ((bf16[4,192,2,512]{3,1,2,0:T(8,128)(2,1)}), bf16[4,192,2,512]{3,1,2,0:T(8,128)(2,1)S(1)}, u32[]{:S(2)}, u32[]{:S(2)}) async-start(bf16[4,192,2,512]{3,1,2,0:T(8,128)(2,1)} %copy.34), calls=%async_computation | async-start | bytes 3145728 | tf_op jit(solution)/shard_map/all_to_all | solution.py:68
  55.3 37.3 %all-to-all-done = bf16[4,192,2,512]{3,1,2,0:T(8,128)(2,1)S(1)} async-done(((bf16[4,192,2,512]{3,1,2,0:T(8,128)(2,1)}), bf16[4,192,2,512]{3,1,2,0:T(8,128)(2,1)S(1)}, u32[]{:S(2)}, u32[]{:S(2)}) %all-to-all-start) | async-done | bytes 1572896 | tf_op jit(solution)/shard_map/all_to_all | solution.py:68
  92.6 3.7 %copy.35 = bf16[1,192,2,4,512]{1,2,4,3,0:T(2,128)(2,1)} copy(bf16[1,192,2,4,512]{4,1,2,3,0:T(8,128)(2,1)S(1)} %bitcast.96) | data formatting | bytes 3145728 | tf_op jit(solution)/shard_map/all_to_all | solution.py:68
  96.4 9.5 %gather_fusion = bf16[2048,192,2]{1,2,0:T(2,128)(2,1)S(1)} fusion(bf16[192,2,2048]{0,1,2:T(2,128)(2,1)} %bitcast.95, s32[2048]{0:T(1024)S(1)} %fusion.15), kind=kCustom, calls=%fused_computation | custom fusion | bytes 3153920 | tf_op jit(solution)/shard_map/jit(_take)/gather | solution.py:69
  105.9 8.1 %broadcast_select_fusion = bf16[1,192,2,2048]{1,2,3,0:T(2,128)(2,1)} fusion(pred[2048]{0:T(1024)(128)(4,1)S(1)} %compare_and_fusion, bf16[2048,192,2]{1,2,0:T(2,128)(2,1)S(1)} %gather_fusion), kind=kLoop, calls=%fused_computation.3 | loop fusion | flops 786432 | bytes 3147776 | tf_op jit(solution)/shard_map/jit(_take)/select_n | solution.py:69
  114.0 6.5 %copy.36 = bf16[192,2,2048]{2,1,0:T(2,128)(2,1)} copy(bf16[192,2,2048]{0,1,2:T(2,128)(2,1)S(1)} %bitcast.94) | data formatting | bytes 3145728 | tf_op jit(solution)/shard_map/jit(_take)/gather | solution.py:69
  120.6 4.0 %gather.7 = bf16[1,192,4096]{2,1,0:T(8,128)(2,1)} reshape(bf16[192,2,2048]{2,1,0:T(2,128)(2,1)} %copy.36) | data formatting | bytes 3145728 | tf_op jit(solution)/shard_map/jit(_take)/gather | solution.py:69
  124.5 6.4 %copy.37 = bf16[1,192,2,2048]{3,2,1,0:T(2,128)(2,1)} copy(bf16[1,192,2,2048]{1,2,3,0:T(2,128)(2,1)S(1)} %copy-done) | data formatting | bytes 3145728 | tf_op jit(solution)/shard_map/jit(_take)/select_n | solution.py:69
  130.9 2.2 %copy.50 = bf16[24,8,2,2048]{3,1,2,0:T(8,128)(2,1)S(1)} copy(bf16[24,8,2,2048]{3,2,1,0:T(2,128)(2,1)} %bitcast.97) | data formatting | bytes 3145728
  133.1 0.0 copy-done.1
  133.1 0.2 broadcast_select_fusion.1
  133.3 0.8 constant_dynamic-slice_fusion
  134.0 5.8 %fusion = bf16[1,1024,4096]{2,1,0:T(8,128)(2,1)} fusion(bf16[192,4096]{1,0:T(8,128)(2,1)S(1)} %bitcast.99, bf16[1,192,4096]{2,1,0:T(8,128)(2,1)S(1)} %broadcast_select_fusion.1, s32[]{:T(128)S(6)} %select_n.165), kind=kOutput, calls=%fused_computation.2 | convolution fusion | flops 1619001344 | bytes 10354692 | tf_op jit(solution)/shard_map/ctr,ctk->crk/dot_general | solution.py:74
  (13 shorter events, 0.1 us)
Async XLA Ops:
  7.2 7.6 %copy-start.2 = (bf16[512,2,1,48]{0,3,2,1:T(8,128)(2,1)S(1)}, bf16[512,2,1,48]{0,3,2,1:T(8,128)(2,1)}, u32[]{:S(2)}) copy-start(bf16[512,2,1,48]{0,3,2,1:T(8,128)(2,1)} %param.4) | copy-start | bytes 294916
  7.2 40.5 %all-gather.3.cloned.1.call-start = ((), (), s32[]{:S(2)}) async-start(), calls=%async_computation.1 | async-start | bytes 1966080 | tf_op jit(solution)/shard_map/all_gather | solution.py:67
  10.8 4.0 %collective-permute-start = (bf16[512,2,1,48]{0,3,1,2:T(8,128)(2,1)S(1)}, bf16[512,2,1,48]{0,3,1,2:T(8,128)(2,1)S(1)}, u32[]{:S(2)}, u32[]{:S(2)}) collective-permute-start(bf16[512,2,1,48]{0,3,1,2:T(8,128)(2,1)S(1)} %slice.45), channel_id=1, source_target_pairs={{0,1},{1,2},{2,3},{4,5},{5,6},{6,7},{8,9},{9,10},{10,11},{12,13},{... | collective-permute-start | bytes 294920 | tf_op jit(solution)/shard_map/ppermute | solution.py:16
  50.5 4.7 %copy-start.3 = (s32[2048]{0:T(1024)S(1)}, s32[2048]{0:T(1024)}, u32[]{:S(2)}) copy-start(s32[2048]{0:T(1024)} %param.5) | copy-start | bytes 24580
  50.5 42.1 %all-to-all-start = ((bf16[4,192,2,512]{3,1,2,0:T(8,128)(2,1)}), bf16[4,192,2,512]{3,1,2,0:T(8,128)(2,1)S(1)}, u32[]{:S(2)}, u32[]{:S(2)}) async-start(bf16[4,192,2,512]{3,1,2,0:T(8,128)(2,1)} %copy.34), calls=%async_computation | async-start | bytes 3145728 | tf_op jit(solution)/shard_map/all_to_all | solution.py:68
  120.5 4.0 %copy-start = (bf16[1,192,2,2048]{1,2,3,0:T(2,128)(2,1)S(1)}, bf16[1,192,2,2048]{1,2,3,0:T(2,128)(2,1)}, u32[]{:S(2)}) copy-start(bf16[1,192,2,2048]{1,2,3,0:T(2,128)(2,1)} %broadcast_select_fusion) | copy-start | bytes 4718596
  130.9 2.2 %copy-start.1 = (bf16[1,192,4096]{2,1,0:T(8,128)(2,1)S(1)}, bf16[1,192,4096]{2,1,0:T(8,128)(2,1)}, u32[]{:S(2)}) copy-start(bf16[1,192,4096]{2,1,0:T(8,128)(2,1)} %gather.7) | copy-start | bytes 4718596
Sparse Core Ops, SparseCore 0:
  23.3 24.2 all-gather.2
where the time goes:
time: 147 us
  waiting for transfers between devices  61.8 us (42%)
  local copies, waits for them, and re-layouts  41.3 us (28%)
  between operations  14.9 us (10%)
  matrix products  12.2 us (8%)
  other arithmetic  9.31 us (6%)
  starting transfers between devices  7.13 us (5%)
    all_to_all x1, waiting for transfers between devices, local(): lax.all_to_all(all_time, 'chan', split_axis=0, concat_axis=3, tiled=True)  37.3 us
    all_gather x1, waiting for transfers between devices, local(): all_time = lax.all_gather(spectrum, 'tblk', axis=1, tiled=True)  24.5 us
    gather x3, local copies, waits for them, and re-layouts, local(): ordered = jnp.take(owned, slot_of_input, axis=3)  20 us
    select_n x2, other arithmetic, local(): ordered = jnp.take(owned, slot_of_input, axis=3)  8.29 us
    dot_general x4, matrix products, channelize(): jnp.einsum('ipctr,prok->cktoi', blocks[:, :, :, step:step + frames, :], t...  6.46 us
    select_n x1, local copies, waits for them, and re-layouts, local(): ordered = jnp.take(owned, slot_of_input, axis=3)  6.37 us
    dot_general x1, matrix products, local(): jnp.einsum('ctr,ctk->crk', tile, series, preferred_element_type=jnp.float32)  5.78 us
    unnamed x10, local copies, waits for them, and re-layouts  5.77 us
  transfers between devices with their start and end apart: 3, of which 2 were waited for; matrix products, arithmetic and copies ran while one was open for 1% of the time, Pallas kernels for 0%

commit v1 on v0

v1 whole, which is shorter than its diff:
```python
import functools
import math

import jax
import jax.numpy as jnp
import ml_dtypes
import numpy as np
from jax import lax
from jax.experimental import pallas as pl
from jax.experimental.pallas import tpu as pltpu
from jax.sharding import PartitionSpec as P

UPCHAN = 16
TAPS = 4
GROUP = 16
PAD = 128
MIB = 1 << 20
VMEM = pl.BlockSpec(memory_space=pltpu.VMEM)
HBM = pl.BlockSpec(memory_space=pltpu.HBM)


def shifted(value, axis, steps):
    count = lax.axis_size(axis)
    leading, last = (max(0, -steps), min(count, count - steps))
    return lax.ppermute(value, axis, [(source, source + steps) for source in range(leading, last)])


def swapped(value, axis, distance):
    count = lax.axis_size(axis)
    return lax.ppermute(value, axis, [(source, source ^ distance) for source in range(count)])


def filter_table(bins):
    length = TAPS * UPCHAN
    taps = np.arange(length)
    center = (length - 1) / 2.0
    window = np.sinc((taps - center) / UPCHAN) * (0.5 - 0.5 * np.cos(2.0 * math.pi * (taps + 0.5) / length))
    window = window / np.sqrt(np.sum(window * window))
    phase = 2.0 * math.pi * ((taps % UPCHAN)[None, :] * np.arange(bins)[:, None] % UPCHAN) / UPCHAN
    cosine, sine = window * np.cos(phase), window * np.sin(phase)
    real = np.stack([cosine, sine], axis=-1)
    imag = np.stack([-sine, cosine], axis=-1)
    return np.stack([real, imag], axis=1).astype(np.float32)


def halves(table):
    high = table.astype(ml_dtypes.bfloat16)
    low = (table - high.astype(np.float32)).astype(ml_dtypes.bfloat16)
    return high, low


def group_table(bins, steps, offset, width, frames):
    taps = filter_table(bins)
    table = np.zeros((bins, 2, frames, 2, width), np.float32)
    for frame in range(steps):
        for tap in range(TAPS * UPCHAN):
            sample = offset + UPCHAN * frame + tap
            if 0 <= sample < width:
                table[:, :, frame, :, sample] = taps[:, :, tap, :]
    high, low = halves(table.reshape(bins, 2 * frames, 2, width))
    return np.stack([high, low], axis=1)


def dot_samples(table, samples):
    return lax.dot_general(table, samples, (((1,), (1,)), ((), ())), preferred_element_type=jnp.float32)


def history_kernel(bins_per_coarse, volts_hbm, table_hbm, tail_ref, samples_ref, table_ref, pairs_ref, sems):
    width = volts_hbm.shape[3]
    rows = table_hbm.shape[2]
    copies = [
        pltpu.make_async_copy(volts_hbm.at[:, :, :, pl.ds(width - PAD, PAD)], samples_ref, sems.at[0]),
        pltpu.make_async_copy(table_hbm, table_ref, sems.at[1]),
    ]
    for copy in copies:
        copy.start()
    for copy in copies:
        copy.wait()
    at = 0
    for coarse, bins in enumerate(bins_per_coarse):
        total = 0.0
        for part, samples in enumerate(parts_of(samples_ref, pairs_ref, coarse, 0)):
            for half in range(2):
                table = table_ref[:bins, half, :, part * PAD : (part + 1) * PAD].reshape(bins * rows, PAD)
                total = total + dot_samples(table, samples)
        tail_ref[at : at + bins * rows, :] = total
        at += bins * rows


def parts_of(samples_ref, pairs_ref, coarse, lane):
    slots = samples_ref.shape[0]
    pairs = samples_ref[:, coarse, :, lane : lane + PAD].reshape(2 * slots, PAD)
    place = lane * 2 * slots // PAD
    pairs_ref[place : place + 2 * slots, :] = pairs.astype(jnp.float32)
    return [pairs_ref[pl.ds(place + part, slots, stride=2), :].astype(jnp.bfloat16) for part in range(2)]


def channel_kernel(plan, volts_ref, lead_ref, table_ref, lead_table_ref, *refs):
    spectrum_refs, early_ref, pairs_ref = refs[:-2], refs[-2], refs[-1]
    slots, _, _, width = volts_ref.shape
    lead_width = lead_ref.shape[2]
    frames = width // UPCHAN
    groups = frames // GROUP
    span = PAD + GROUP * UPCHAN
    first = lax.axis_index("tblk") == 0
    me = lax.axis_index("chan")
    for coarse, members in plan:
        bins = [lax.bitwise_xor(me, distance) if relative else distance for relative, distance, _ in members]
        count = len(bins)
        table = [table_ref[pl.ds(k, 1), half] for half in range(2) for k in bins]
        table = jnp.concatenate(table, axis=0).reshape(2 * count * 2 * GROUP, 2 * span)
        lead_table = [lead_table_ref[pl.ds(k, 1), half] for half in range(2) for k in bins]
        lead_table = jnp.concatenate(lead_table, axis=0).reshape(2 * count * 8, 2 * lead_width)
        head = 0.0
        for part in range(2):
            lead = lead_ref[part, coarse, :, :]
            head = head + jnp.dot(
                lead_table[:, part * lead_width : (part + 1) * lead_width], lead, preferred_element_type=jnp.float32
            )
        head = jnp.where(first, head[: count * 8] + head[count * 8 :], 0.0).reshape(count, 2, 4, slots)
        samples = [parts_of(volts_ref, pairs_ref, coarse, lane) for lane in range(0, width, PAD)]
        for group in range(groups):
            total = 0.0
            for lane in range(span // PAD):
                at = group * GROUP * UPCHAN // PAD - 1 + lane
                if at < 0:
                    continue
                for part in range(2):
                    columns = part * span + lane * PAD
                    total = total + dot_samples(table[:, columns : columns + PAD], samples[at][part])
            total = total.reshape(2, count, 2, GROUP, slots)
            total = total[0] + total[1]
            if group == 0:
                opening = total[:, :, :4, :] + head
                row = (coarse * UPCHAN) * 8
                early_ref[row : row + count * 8, :] = opening.reshape(count * 8, slots)
            for at, (_, _, (out, index)) in enumerate(members):
                for part in range(2):
                    row = part * frames + group * GROUP
                    spectrum_refs[out][index, row : row + GROUP, :] = total[at, part].astype(jnp.bfloat16)


def early_kernel(plan, early_ref, history_ref, *refs):
    spectra_in, spectra_out = refs[: len(refs) // 2], refs[len(refs) // 2 :]
    me = lax.axis_index("chan")
    for coarse, members in plan:
        for at, (relative, distance, (out, index)) in enumerate(members):
            frames = spectra_in[out].shape[1] // 2
            bin_at = (lax.bitwise_xor(me, distance) if relative else distance) + coarse * UPCHAN
            row = (coarse * UPCHAN + at) * 8
            total = early_ref[row : row + 8, :] + history_ref[pl.ds(pl.multiple_of(bin_at * 8, 8), 8), :]
            for part in range(2):
                opening = total if part == 0 else pltpu.roll(total, 4, 0)
                opening = jnp.concatenate([opening, opening], axis=0)
                old = spectra_in[out][index, part * frames : part * frames + GROUP, :].astype(jnp.float32)
                row = lax.broadcasted_iota(jnp.int32, old.shape, 0)
                new = jnp.where(row < 4, opening, old).astype(jnp.bfloat16)
                spectra_out[out][index, part * frames : part * frames + GROUP, :] = new


def choice_kernel(relative, source, slots, slot_ref, choice_ref):
    owner = lax.bitwise_xor(lax.axis_index("chan"), source) if relative else source
    for row in range(0, choice_ref.shape[0], 64):
        rows = min(64, choice_ref.shape[0] - row)
        place = lax.broadcasted_iota(jnp.int32, (rows, slot_ref.shape[1]), 0) + (owner * slots + row)
        choice_ref[row : row + rows, :] = (place == slot_ref[...]).astype(jnp.bfloat16)


def order_kernel(places, fresh, choice_ref, *refs):
    pieces, old_ref, new_ref = refs[: len(places)], refs[-2], refs[-1]
    put_in_order(places, fresh, choice_ref, pieces, old_ref, new_ref)


def put_in_order(places, fresh, choice_ref, pieces, old_ref, new_ref):
    rows = pieces[0].shape[0]
    frames = rows // 2
    inputs = choice_ref.shape[1]
    stacked = jnp.concatenate([piece[...] for piece in pieces], axis=0)
    for column in range(0, inputs, 256):
        total = jnp.dot(stacked, choice_ref[:, column : column + 256], preferred_element_type=jnp.float32)
        total = total.astype(jnp.bfloat16)
        for at, place in enumerate(places):
            for part in range(2):
                value = total[at * rows + part * frames : at * rows + (part + 1) * frames]
                to = (slice(place * frames, (place + 1) * frames), slice(part * inputs + column, part * inputs + column + 256))
                new_ref[to] = value if fresh else old_ref[to] + value


def gram_kernel(blocks, relative, places, choice_ref, *refs):
    pieces, old_ref = refs[: len(places)], refs[len(places)]
    fine_hbm, gram_hbm, ordered, tile, result, sems = refs[len(places) + 1 :]
    frames = ordered.shape[0] // blocks
    width = tile.shape[0]
    own = 0 if relative else pl.multiple_of(lax.axis_index("tblk") * frames, frames)
    if places:
        inside = [place for place in range(blocks) if place not in places]
        for place in inside:
            ordered[place * frames : (place + 1) * frames, :] = old_ref[place * frames : (place + 1) * frames, :]
        put_in_order(places, False, choice_ref, pieces, old_ref, ordered)
    else:
        ordered[...] = old_ref[...]
    copies = [pltpu.make_async_copy(ordered.at[pl.ds(own, frames), :], fine_hbm, sems.at[0])]
    copies[0].start()
    place = pl.multiple_of(lax.axis_index("tblk") * width, width)
    tile[...] = ordered[:, pl.ds(place, width)].T
    chunk = width // 8
    for at in range(8):
        rows = slice(at * chunk, (at + 1) * chunk)
        gram = jnp.dot(tile[rows, :], ordered[...], preferred_element_type=jnp.float32)
        result[rows, :] = (gram * (1.0 / ordered.shape[0])).astype(jnp.bfloat16)
        copy = pltpu.make_async_copy(
            result.at[pl.ds(at * chunk, chunk), :], gram_hbm.at[pl.ds(at * chunk, chunk), :], sems.at[at + 1]
        )
        copy.start()
        copies.append(copy)
    for copy in copies:
        copy.wait()


def call(kernel, shapes, *operands, name, limit, spaces=VMEM, outs=VMEM, **options):
    spaces = spaces if isinstance(spaces, list) else [spaces] * len(operands)
    several = isinstance(shapes, list)
    return pl.pallas_call(
        kernel,
        in_specs=spaces,
        out_specs=[outs] * len(shapes) if several else outs,
        out_shape=shapes,
        compiler_params=pltpu.CompilerParams(vmem_limit_bytes=limit * MIB),
        name=name,
        **options,
    )(*operands)


def local(coarse_volts, lead_in, slot_of_input):
    slots, _, coarse, width = coarse_volts.shape
    lead_width = lead_in.shape[3]
    chans, blocks = lax.axis_size("chan"), lax.axis_size("tblk")
    frames = width // UPCHAN
    inputs = slot_of_input.shape[0]
    relative = coarse == 1 and chans == 4 and blocks == 4
    volts = coarse_volts.transpose(0, 2, 1, 3)
    lead = lead_in.transpose(1, 2, 3, 0)
    order = slot_of_input.reshape(1, inputs)

    per_coarse = [max(0, min(UPCHAN, chans - c * UPCHAN)) for c in range(coarse)]
    bins = max(per_coarse)
    span = PAD + GROUP * UPCHAN
    main = group_table(bins, GROUP, PAD - lead_width, span, GROUP)
    tail = group_table(bins, TAPS - 1, PAD - lead_width, PAD, 4)
    head = group_table(bins, TAPS - 1, 0, lead_width, 4)
    main, tail, head = (jnp.asarray(t.reshape(t.shape[:3] + (-1,))) for t in (main, tail, head))
    shape = jax.ShapeDtypeStruct

    opening = call(
        functools.partial(history_kernel, per_coarse),
        shape((chans * 8, slots), jnp.float32),
        volts,
        tail,
        name="history",
        limit=4,
        spaces=HBM,
        scratch_shapes=[
            pltpu.VMEM((slots, coarse, 2, PAD), jnp.bfloat16),
            pltpu.VMEM(tail.shape, jnp.bfloat16),
            pltpu.VMEM((2 * slots, PAD), jnp.float32),
            pltpu.SemaphoreType.DMA((2,)),
        ],
    )
    history = shifted(opening, "tblk", 1)

    if relative:
        plan = [(0, [(True, distance, (distance, 0)) for distance in range(chans)])]
        shapes = [shape((1, 2 * frames, slots), jnp.bfloat16)] * chans
    else:
        plan = [
            (c, [(False, k, (0, c * UPCHAN + k)) for k in range(count)]) for c, count in enumerate(per_coarse) if count
        ]
        shapes = [shape((chans, 2 * frames, slots), jnp.bfloat16)]
    *spectra, early = call(
        functools.partial(channel_kernel, plan),
        shapes + [shape((chans * 8, slots), jnp.float32)],
        volts,
        lead,
        main,
        head,
        name="channelize",
        limit=14,
        scratch_shapes=[pltpu.VMEM((2 * slots * width // PAD, PAD), jnp.float32)],
    )
    spectra = call(
        functools.partial(early_kernel, plan),
        shapes,
        early,
        history,
        *spectra,
        name="early",
        limit=2,
        input_output_aliases={2 + at: at for at in range(len(shapes))},
    )

    if relative:
        spectra = [s[0] for s in spectra]
        near = [spectra[0]] + [swapped(spectra[d], "chan", d) for d in (1, 2, 3)]
        pieces = []
        for piece in near:
            far = swapped(piece, "tblk", 2)
            pieces.append([piece, swapped(piece, "tblk", 1), far, swapped(far, "tblk", 1)])
    else:
        owned = lax.all_to_all(spectra[0], "chan", split_axis=0, concat_axis=2, tiled=True)[0]
        all_time = lax.all_gather(owned, "tblk", axis=0)
        pieces = [[all_time[b] for b in range(blocks)]]
        slots = inputs

    choices = [
        call(
            functools.partial(choice_kernel, relative, source, slots),
            shape((slots, inputs), jnp.bfloat16),
            order,
            name="choice",
            limit=2 if relative else 10,
        )
        for source in range(len(pieces))
    ]
    ordered_shape = shape((blocks * frames, 2 * inputs), jnp.bfloat16)
    ordered = jnp.zeros(ordered_shape.shape, ordered_shape.dtype)
    if relative:
        for source in range(3):
            ordered = call(
                functools.partial(order_kernel, list(range(blocks)), source == 0),
                ordered_shape,
                choices[source],
                *pieces[source],
                ordered,
                name="order",
                limit=6,
                input_output_aliases={1 + blocks: 0},
            )
        ordered = call(
            functools.partial(order_kernel, [0, 1], False),
            ordered_shape,
            choices[3],
            *pieces[3][:2],
            ordered,
            name="order",
            limit=6,
            input_output_aliases={3: 0},
        )
        places, last, choice = [2, 3], pieces[3][2:], choices[3]
    else:
        places, last, choice = list(range(blocks)), pieces[0], choices[0]

    tile_rows = 2 * inputs // blocks
    fine, gram = call(
        functools.partial(gram_kernel, blocks, relative, places),
        [shape((frames, 2 * inputs), jnp.bfloat16), shape((tile_rows, 2 * inputs), jnp.bfloat16)],
        choice,
        *last,
        ordered,
        name="gram",
        limit=20 if relative else 40,
        outs=HBM,
        scratch_shapes=[
            pltpu.VMEM(ordered_shape.shape, jnp.bfloat16),
            pltpu.VMEM((tile_rows, blocks * frames), jnp.bfloat16),
            pltpu.VMEM((tile_rows, 2 * inputs), jnp.bfloat16),
            pltpu.SemaphoreType.DMA((9,)),
        ],
    )
    return fine[None], gram[None]


def solution(mesh):
    placed = (P("chan", None, "grp", "tblk"), P("chan", None, "grp", None), P())
    return jax.shard_map(
        local,
        mesh=mesh,
        in_specs=placed,
        out_specs=(P(("grp", "chan"), "tblk", None), P(("grp", "chan"), "tblk", None)),
        check_vma=False,
    )
```

time: 147 us -> 39.4 us (0.27)
  waiting for transfers between devices: 61.8 us -> 8.88 us
  local copies, waits for them, and re-layouts: 41.3 us -> 4.21 us
  between operations: 14.9 us -> 0.83 us
  matrix products: 12.2 us -> 0 us
  Pallas kernels: 0 us -> 12.2 us
  other arithmetic: 9.31 us -> 0 us
  starting transfers between devices: 7.13 us -> 13 us
    all_to_all x1 -> x0, waiting for transfers between devices: 37.3 us -> none  [local(): lax.all_to_all(all_time, 'chan', split_axis=0, concat_axis=3, tiled=True)]
    all_gather x1 -> x0, waiting for transfers between devices: 24.5 us -> none  [local(): all_time = lax.all_gather(spectrum, 'tblk', axis=1, tiled=True)]
    gather x3 -> x0, local copies, waits for them, and re-layouts: 20 us -> none  [local(): ordered = jnp.take(owned, slot_of_input, axis=3)]
    dot_general x5 -> x0, matrix products: 12.2 us -> none  [the longest x4 6.46 us: channelize(): jnp.einsum('ipctr,prok->cktoi', blocks[:, :, :, step:step + frames, :], t...]
    pallas_call x0 -> x12, Pallas kernels: none -> 12.2 us  [call(): pl.pallas_call(kernel, in_specs=spaces, out_specs=[outs] * len(shapes) if...]
    ppermute x0 -> x15, starting transfers between devices: none -> 10.6 us  [swapped(): lax.ppermute(value, axis, [(source, source ^ distance) for source in rang...]
    ppermute x0 -> x15, waiting for transfers between devices: none -> 8.88 us  [swapped(): lax.ppermute(value, axis, [(source, source ^ distance) for source in rang...]
    select_n x4 -> x0, other arithmetic: 8.32 us -> none  [the longest x2 8.29 us: local(): ordered = jnp.take(owned, slot_of_input, axis=3)]
  transfers between devices with their start and end apart: 3 -> 16, of which waited for: 2 -> 5; matrix products, arithmetic and copies ran while one was open for 1% -> 0% of each run, Pallas kernels for 0% -> 18%
where the time goes in v1:
time: 39.4 us; the launch traced here: 39.1 us
  starting transfers between devices  13 us (33%)
  Pallas kernels  12.2 us (31%)
  waiting for transfers between devices  8.88 us (23%)
  local copies, waits for them, and re-layouts  4.21 us (11%)
  between operations  0.83 us (2%)
    pallas_call x12, Pallas kernels, call(): pl.pallas_call(kernel, in_specs=spaces, out_specs=[outs] * len(shapes) if...  12.2 us
    ppermute x15, starting transfers between devices, swapped(): lax.ppermute(value, axis, [(source, source ^ distance) for source in rang...  10.6 us
    ppermute x15, waiting for transfers between devices, swapped(): lax.ppermute(value, axis, [(source, source ^ distance) for source in rang...  8.88 us
    unnamed x14, local copies, waits for them, and re-layouts  4.05 us
    ppermute x1, starting transfers between devices, shifted(): lax.ppermute(value, axis, [(source, source + steps) for source in range(l...  2.36 us
  transfers between devices with their start and end apart: 16, of which 5 were waited for; matrix products, arithmetic and copies ran while one was open for 0% of the time, Pallas kernels for 18%

profile of v1, /device:TPU:0, one launch (start us, length us, event | category | flops | bytes accessed | tf_op | source)
XLA Modules:
  0.0 39.1 jit_solution(5225697128678885357)
XLA Ops:
  0.6 1.4 %copy-done = bf16[512,2,1,768]{3,1,2,0:T(2,128)(2,1)S(1)} copy-done((bf16[512,2,1,768]{3,1,2,0:T(2,128)(2,1)S(1)}, bf16[512,2,1,768]{3,1,2,0:T(2,128)(2,1)}, u32[]{:S(2)}) %copy-start) | copy-done | bytes 1572888
  2.0 0.8 %copy-done.5 = bf16[4,2,8,256]{3,2,1,0:T(8,128)(2,1)S(1)} copy-done((bf16[4,2,8,256]{3,2,1,0:T(8,128)(2,1)S(1)}, bf16[4,2,8,256]{3,2,1,0:T(8,128)(2,1)}, u32[]{:S(2)}) %copy-start.5) | copy-done | bytes 32792
  2.8 0.7 %history.1 = f32[32,512]{1,0:T(8,128)S(1)} custom-call(bf16[512,1,2,768]{3,2,1,0:T(2,128)(2,1)S(1)} %bitcast.9, bf16[4,2,8,256]{3,2,1,0:T(8,128)(2,1)S(1)} %copy-done.5), custom_call_target="tpu_custom_call" | custom-call | tf_op jit(solution)/shard_map/history/pallas_call | solution.py:223
  3.5 2.4 %collective-permute-start = (f32[32,512]{1,0:T(8,128)S(1)}, f32[32,512]{1,0:T(8,128)S(1)}, u32[]{:S(2)}, u32[]{:S(2)}) collective-permute-start(f32[32,512]{1,0:T(8,128)S(1)} %history.1), channel_id=1, source_target_pairs={{0,1},{1,2},{2,3},{4,5},{5,6},{6,7},{8,9},{9,10},{10,11},{12,13},{... | collective-permute-start | bytes 196616 | tf_op jit(solution)/shard_map/ppermute | solution.py:25
  5.9 0.0 copy-start.2
  5.9 1.0 %copy-done.2 = bf16[4,2,32,768]{3,2,1,0:T(8,128)(2,1)S(1)} copy-done((bf16[4,2,32,768]{3,2,1,0:T(8,128)(2,1)S(1)}, bf16[4,2,32,768]{3,2,1,0:T(8,128)(2,1)}, u32[]{:S(2)}) %copy-start.2) | copy-done | bytes 393240
  6.9 0.9 %copy-done.4 = bf16[512,2,1,48]{0,3,2,1:T(8,128)(2,1)S(1)} copy-done((bf16[512,2,1,48]{0,3,2,1:T(8,128)(2,1)S(1)}, bf16[512,2,1,48]{0,3,2,1:T(8,128)(2,1)}, u32[]{:S(2)}) %copy-start.4) | copy-done | bytes 98328
  7.8 2.0 %channelize.1 = (bf16[1,96,512]{2,1,0:T(8,128)(2,1)S(1)}, bf16[1,96,512]{2,1,0:T(8,128)(2,1)S(1)}, bf16[1,96,512]{2,1,0:T(8,128)(2,1)S(1)}, bf16[1,96,512]{2,1,0:T(8,128)(2,1)S(1)}, f32[32,512]{1,0:T(8,128)S(1)}) custom-call(bf16[512,1,2,768]{3,2,1,0:T(2,128)(2,1)S(1)} %bitcast.10, bf16[2,1,48,512]{3,2,1,0:T(8,128)(2,1)S(1)} %bitcast.18, ...), custom_call_target="tpu_custom_call" | custom-call | tf_op jit(solution)/shard_map/channelize/pallas_call | solution.py:223
  9.8 3.5 %collective-permute-start.5 = (bf16[96,512]{1,0:T(8,128)(2,1)S(1)}, bf16[96,512]{1,0:T(8,128)(2,1)S(1)}, u32[]{:S(2)}, u32[]{:S(2)}) collective-permute-start(bf16[96,512]{1,0:T(8,128)(2,1)S(1)} %bitcast.20), channel_id=1, source_target_pairs={{0,8},{4,12},{8,0},{12,4},{1,9},{5,13},{9,1},{13,5},{2,10},{6,14},... | collective-permute-start | bytes 294920 | tf_op jit(solution)/shard_map/ppermute | solution.py:30
  13.3 1.6 %collective-permute-start.9 = (bf16[96,512]{1,0:T(8,128)(2,1)S(1)}, bf16[96,512]{1,0:T(8,128)(2,1)S(1)}, u32[]{:S(2)}, u32[]{:S(2)}) collective-permute-start(bf16[96,512]{1,0:T(8,128)(2,1)S(1)} %bitcast.19), channel_id=1, source_target_pairs={{0,4},{4,0},{8,12},{12,8},{1,5},{5,1},{9,13},{13,9},{2,6},{6,2},{1... | collective-permute-start | bytes 294920 | tf_op jit(solution)/shard_map/ppermute | solution.py:30
  14.9 1.9 %collective-permute-start.14 = (bf16[96,512]{1,0:T(8,128)(2,1)S(1)}, bf16[96,512]{1,0:T(8,128)(2,1)S(1)}, u32[]{:S(2)}, u32[]{:S(2)}) collective-permute-start(bf16[96,512]{1,0:T(8,128)(2,1)S(1)} %bitcast.11), channel_id=1, source_target_pairs={{0,2},{1,3},{2,0},{3,1},{4,6},{5,7},{6,4},{7,5},{8,10},{9,11},{10,... | collective-permute-start | bytes 294920 | tf_op jit(solution)/shard_map/ppermute | solution.py:30
  16.8 2.3 %collective-permute-done.9.refs_0_ = bf16[96,512]{1,0:T(8,128)(2,1)S(1)} collective-permute-done((bf16[96,512]{1,0:T(8,128)(2,1)S(1)}, bf16[96,512]{1,0:T(8,128)(2,1)S(1)}, u32[]{:S(2)}, u32[]{:S(2)}) %collective-permute-start.9) | collective-permute-done | bytes 98336 | tf_op jit(solution)/shard_map/ppermute | solution.py:30
  19.0 0.9 %collective-permute-start.11 = (bf16[96,512]{1,0:T(8,128)(2,1)S(1)}, bf16[96,512]{1,0:T(8,128)(2,1)S(1)}, u32[]{:S(2)}, u32[]{:S(2)}) collective-permute-start(bf16[96,512]{1,0:T(8,128)(2,1)S(1)} %collective-permute-done.9.refs_0_), channel_id=1, source_target_pairs={{0,2},{1,3},{2,0},{3,1},{4,6},{5,7},{6,4},{7,5},{8,10},{9,11},{10,... | collective-permute-start | bytes 294920 | tf_op jit(solution)/shard_map/ppermute | solution.py:30
  19.9 1.1 %collective-permute-start.7 = (bf16[96,512]{1,0:T(8,128)(2,1)S(1)}, bf16[96,512]{1,0:T(8,128)(2,1)S(1)}, u32[]{:S(2)}, u32[]{:S(2)}) collective-permute-start(bf16[96,512]{1,0:T(8,128)(2,1)S(1)} %collective-permute-done.5.refs_0_), channel_id=1, source_target_pairs={{0,2},{1,3},{2,0},{3,1},{4,6},{5,7},{6,4},{7,5},{8,10},{9,11},{10,... | collective-permute-start | bytes 294920 | tf_op jit(solution)/shard_map/ppermute | solution.py:30
  21.1 1.4 %collective-permute-done.1.refs_0_ = bf16[96,512]{1,0:T(8,128)(2,1)S(1)} collective-permute-done((bf16[96,512]{1,0:T(8,128)(2,1)S(1)}, bf16[96,512]{1,0:T(8,128)(2,1)S(1)}, u32[]{:S(2)}, u32[]{:S(2)}) %collective-permute-start.1) | collective-permute-done | bytes 98336 | tf_op jit(solution)/shard_map/ppermute | solution.py:30
  22.5 0.6 %collective-permute-start.2 = (bf16[96,512]{1,0:T(8,128)(2,1)S(1)}, bf16[96,512]{1,0:T(8,128)(2,1)S(1)}, u32[]{:S(2)}, u32[]{:S(2)}) collective-permute-start(bf16[96,512]{1,0:T(8,128)(2,1)S(1)} %collective-permute-done.1.refs_0_), channel_id=1, source_target_pairs={{0,2},{1,3},{2,0},{3,1},{4,6},{5,7},{6,4},{7,5},{8,10},{9,11},{10,... | collective-permute-start | bytes 294920 | tf_op jit(solution)/shard_map/ppermute | solution.py:30
  23.1 0.5 %collective-permute-start.15 = (bf16[96,512]{1,0:T(8,128)(2,1)S(1)}, bf16[96,512]{1,0:T(8,128)(2,1)S(1)}, u32[]{:S(2)}, u32[]{:S(2)}) collective-permute-start(bf16[96,512]{1,0:T(8,128)(2,1)S(1)} %collective-permute-done.14.refs_2_), channel_id=1, source_target_pairs={{0,1},{1,0},{2,3},{3,2},{4,5},{5,4},{6,7},{7,6},{8,9},{9,8},{10,11... | collective-permute-start | bytes 294920 | tf_op jit(solution)/shard_map/ppermute | solution.py:30
  23.6 1.1 %collective-permute-done.11.refs_2_ = bf16[96,512]{1,0:T(8,128)(2,1)S(1)} collective-permute-done((bf16[96,512]{1,0:T(8,128)(2,1)S(1)}, bf16[96,512]{1,0:T(8,128)(2,1)S(1)}, u32[]{:S(2)}, u32[]{:S(2)}) %collective-permute-start.11) | collective-permute-done | bytes 98336 | tf_op jit(solution)/shard_map/ppermute | solution.py:30
  24.7 2.1 %collective-permute-done.7.refs_2_ = bf16[96,512]{1,0:T(8,128)(2,1)S(1)} collective-permute-done((bf16[96,512]{1,0:T(8,128)(2,1)S(1)}, bf16[96,512]{1,0:T(8,128)(2,1)S(1)}, u32[]{:S(2)}, u32[]{:S(2)}) %collective-permute-start.7) | collective-permute-done | bytes 98336 | tf_op jit(solution)/shard_map/ppermute | solution.py:30
  26.8 1.9 %collective-permute-done.2.refs_0_ = bf16[96,512]{1,0:T(8,128)(2,1)S(1)} collective-permute-done((bf16[96,512]{1,0:T(8,128)(2,1)S(1)}, bf16[96,512]{1,0:T(8,128)(2,1)S(1)}, u32[]{:S(2)}, u32[]{:S(2)}) %collective-permute-start.2) | collective-permute-done | bytes 98336 | tf_op jit(solution)/shard_map/ppermute | solution.py:30
  28.7 0.5 %collective-permute-start.4 = (bf16[96,512]{1,0:T(8,128)(2,1)S(1)}, bf16[96,512]{1,0:T(8,128)(2,1)S(1)}, u32[]{:S(2)}, u32[]{:S(2)}) collective-permute-start(bf16[96,512]{1,0:T(8,128)(2,1)S(1)} %collective-permute-done.1.refs_0_), channel_id=1, source_target_pairs={{0,1},{1,0},{2,3},{3,2},{4,5},{5,4},{6,7},{7,6},{8,9},{9,8},{10,11... | collective-permute-start | bytes 294920 | tf_op jit(solution)/shard_map/ppermute | solution.py:30
  29.2 0.1 collective-permute-start.3
  29.3 0.4 choice.4.choice_ref
  29.7 0.4 choice.7.choice_ref
  30.0 0.4 choice.6.choice_ref
  30.4 0.4 choice.5.choice_ref
  30.8 0.2 broadcast_in_dim.9.refs_4_
  31.0 1.0 %order.4.refs_4_ = bf16[192,4096]{1,0:T(8,128)(2,1)S(1)} custom-call(bf16[512,2048]{1,0:T(8,128)(2,1)S(1)} %choice.7.choice_ref, bf16[96,512]{1,0:T(8,128)(2,1)S(1)} %bitcast.13, bf16[96,512]{1,0:T(8,128)(2,1)S(1)} %collective-permute-done.13.refs_1_, bf16[96,512]{1,0:T(8,128)(2,1)S(1)} %collective-permute-done.14.refs_2_, ...), custom_call_target="tpu_custom_call", output_to_operand_aliasing={{}: (5, {})} | custom-call | tf_op jit(solution)/shard_map/order/pallas_call | solution.py:223
  32.0 1.0 %order.5.refs_4_ = bf16[192,4096]{1,0:T(8,128)(2,1)S(1)} custom-call(bf16[512,2048]{1,0:T(8,128)(2,1)S(1)} %choice.6.choice_ref, bf16[96,512]{1,0:T(8,128)(2,1)S(1)} %collective-permute-done.9.refs_0_, bf16[96,512]{1,0:T(8,128)(2,1)S(1)} %collective-permute-done.10.refs_1_, ...), custom_call_target="tpu_custom_call", output_to_operand_aliasing={{}: (5, {})} | custom-call | tf_op jit(solution)/shard_map/order/pallas_call | solution.py:223
  33.0 1.0 %order.6.refs_2_ = bf16[192,4096]{1,0:T(8,128)(2,1)S(1)} custom-call(bf16[512,2048]{1,0:T(8,128)(2,1)S(1)} %choice.5.choice_ref, bf16[96,512]{1,0:T(8,128)(2,1)S(1)} %collective-permute-done.5.refs_0_, bf16[96,512]{1,0:T(8,128)(2,1)S(1)} %collective-permute-done.6.refs_1_, ...), custom_call_target="tpu_custom_call", output_to_operand_aliasing={{}: (5, {})} | custom-call | tf_op jit(solution)/shard_map/order/pallas_call | solution.py:223
  34.0 0.6 %order.7.refs_2_ = bf16[192,4096]{1,0:T(8,128)(2,1)S(1)} custom-call(bf16[512,2048]{1,0:T(8,128)(2,1)S(1)} %choice.4.choice_ref, bf16[96,512]{1,0:T(8,128)(2,1)S(1)} %collective-permute-done.1.refs_0_, bf16[96,512]{1,0:T(8,128)(2,1)S(1)} %collective-permute-done.4.refs_1_, bf16[192,4096]{1,0:T(8,128)(2,1)S(1)} %order.6.refs_2_), custom_call_target="tpu_custom_call", output_to_operand_aliasing={{}: (3, {})} | custom-call | tf_op jit(solution)/shard_map/order/pallas_call | solution.py:223
  34.7 4.4 %gram.1 = (bf16[48,4096]{1,0:T(8,128)(2,1)}, bf16[1024,4096]{1,0:T(8,128)(2,1)}) custom-call(bf16[512,2048]{1,0:T(8,128)(2,1)S(1)} %choice.4.choice_ref, bf16[96,512]{1,0:T(8,128)(2,1)S(1)} %collective-permute-done.2.refs_0_, bf16[96,512]{1,0:T(8,128)(2,1)S(1)} %collective-permute-done.3.refs_1_, bf16[192,4096]{1,0:T(8,128)(2,1)S(1)} %order.7.refs_2_), custom_call_target="tpu_custom_call" | custom-call | tf_op jit(solution)/shard_map/gram/pallas_call | solution.py:223
  (27 shorter events, 0.1 us)
Async XLA Ops:
  0.6 1.4 %copy-start = (bf16[512,2,1,768]{3,1,2,0:T(2,128)(2,1)S(1)}, bf16[512,2,1,768]{3,1,2,0:T(2,128)(2,1)}, u32[]{:S(2)}) copy-start(bf16[512,2,1,768]{3,1,2,0:T(2,128)(2,1)} %param.6) | copy-start | bytes 4718596
  2.0 0.8 %copy-start.5 = (bf16[4,2,8,256]{3,2,1,0:T(8,128)(2,1)S(1)}, bf16[4,2,8,256]{3,2,1,0:T(8,128)(2,1)}, u32[]{:S(2)}) copy-start(bf16[4,2,8,256]{3,2,1,0:T(8,128)(2,1)} %constant.9.clone.table_hbm) | copy-start | bytes 98308
  2.8 3.1 %copy-start.1 = (bf16[512,2,1,768]{3,1,2,0:T(2,128)(2,1)S(1)}, bf16[512,2,1,768]{3,1,2,0:T(2,128)(2,1)}, u32[]{:S(2)}) copy-start(bf16[512,2,1,768]{3,1,2,0:T(2,128)(2,1)} %param.6) | copy-start | bytes 4718596
  2.8 3.1 %copy-start.6 = (bf16[4,2,8,96]{3,2,1,0:T(8,128)(2,1)S(1)}, bf16[4,2,8,96]{3,2,1,0:T(8,128)(2,1)}, u32[]{:S(2)}) copy-start(bf16[4,2,8,96]{3,2,1,0:T(8,128)(2,1)} %constant.10.clone.lead_table_ref) | copy-start | bytes 36868
  2.8 26.5 %copy-start.3 = (s32[2048]{0:T(1024)S(1)}, s32[2048]{0:T(1024)}, u32[]{:S(2)}) copy-start(s32[2048]{0:T(1024)} %param.8) | copy-start | bytes 24580
  3.5 6.3 %collective-permute-start = (f32[32,512]{1,0:T(8,128)S(1)}, f32[32,512]{1,0:T(8,128)S(1)}, u32[]{:S(2)}, u32[]{:S(2)}) collective-permute-start(f32[32,512]{1,0:T(8,128)S(1)} %history.1), channel_id=1, source_target_pairs={{0,1},{1,2},{2,3},{4,5},{5,6},{6,7},{8,9},{9,10},{10,11},{12,13},{... | collective-permute-start | bytes 196616 | tf_op jit(solution)/shard_map/ppermute | solution.py:25
  5.9 1.0 %copy-start.2 = (bf16[4,2,32,768]{3,2,1,0:T(8,128)(2,1)S(1)}, bf16[4,2,32,768]{3,2,1,0:T(8,128)(2,1)}, u32[]{:S(2)}) copy-start(bf16[4,2,32,768]{3,2,1,0:T(8,128)(2,1)} %constant.8.clone.table_ref) | copy-start | bytes 1179652
  6.9 0.9 %copy-start.4 = (bf16[512,2,1,48]{0,3,2,1:T(8,128)(2,1)S(1)}, bf16[512,2,1,48]{0,3,2,1:T(8,128)(2,1)}, u32[]{:S(2)}) copy-start(bf16[512,2,1,48]{0,3,2,1:T(8,128)(2,1)} %param.7) | copy-start | bytes 294916
  9.8 10.1 %collective-permute-start.5 = (bf16[96,512]{1,0:T(8,128)(2,1)S(1)}, bf16[96,512]{1,0:T(8,128)(2,1)S(1)}, u32[]{:S(2)}, u32[]{:S(2)}) collective-permute-start(bf16[96,512]{1,0:T(8,128)(2,1)S(1)} %bitcast.20), channel_id=1, source_target_pairs={{0,8},{4,12},{8,0},{12,4},{1,9},{5,13},{9,1},{13,5},{2,10},{6,14},... | collective-permute-start | bytes 294920 | tf_op jit(solution)/shard_map/ppermute | solution.py:30
  13.3 5.8 %collective-permute-start.9 = (bf16[96,512]{1,0:T(8,128)(2,1)S(1)}, bf16[96,512]{1,0:T(8,128)(2,1)S(1)}, u32[]{:S(2)}, u32[]{:S(2)}) collective-permute-start(bf16[96,512]{1,0:T(8,128)(2,1)S(1)} %bitcast.19), channel_id=1, source_target_pairs={{0,4},{4,0},{8,12},{12,8},{1,5},{5,1},{9,13},{13,9},{2,6},{6,2},{1... | collective-permute-start | bytes 294920 | tf_op jit(solution)/shard_map/ppermute | solution.py:30
  14.9 7.6 %collective-permute-start.1 = (bf16[96,512]{1,0:T(8,128)(2,1)S(1)}, bf16[96,512]{1,0:T(8,128)(2,1)S(1)}, u32[]{:S(2)}, u32[]{:S(2)}) collective-permute-start(bf16[96,512]{1,0:T(8,128)(2,1)S(1)} %bitcast.21), channel_id=1, source_target_pairs={{0,12},{4,8},{8,4},{12,0},{1,13},{5,9},{9,5},{13,1},{2,14},{6,10},... | collective-permute-start | bytes 294920 | tf_op jit(solution)/shard_map/ppermute | solution.py:30
  14.9 8.2 %collective-permute-start.14 = (bf16[96,512]{1,0:T(8,128)(2,1)S(1)}, bf16[96,512]{1,0:T(8,128)(2,1)S(1)}, u32[]{:S(2)}, u32[]{:S(2)}) collective-permute-start(bf16[96,512]{1,0:T(8,128)(2,1)S(1)} %bitcast.11), channel_id=1, source_target_pairs={{0,2},{1,3},{2,0},{3,1},{4,6},{5,7},{6,4},{7,5},{8,10},{9,11},{10,... | collective-permute-start | bytes 294920 | tf_op jit(solution)/shard_map/ppermute | solution.py:30
  16.8 6.3 %collective-permute-start.13 = (bf16[96,512]{1,0:T(8,128)(2,1)S(1)}, bf16[96,512]{1,0:T(8,128)(2,1)S(1)}, u32[]{:S(2)}, u32[]{:S(2)}) collective-permute-start(bf16[96,512]{1,0:T(8,128)(2,1)S(1)} %bitcast.12), channel_id=1, source_target_pairs={{0,1},{1,0},{2,3},{3,2},{4,5},{5,4},{6,7},{7,6},{8,9},{9,8},{10,11... | collective-permute-start | bytes 294920 | tf_op jit(solution)/shard_map/ppermute | solution.py:30
  19.0 5.7 %collective-permute-start.11 = (bf16[96,512]{1,0:T(8,128)(2,1)S(1)}, bf16[96,512]{1,0:T(8,128)(2,1)S(1)}, u32[]{:S(2)}, u32[]{:S(2)}) collective-permute-start(bf16[96,512]{1,0:T(8,128)(2,1)S(1)} %collective-permute-done.9.refs_0_), channel_id=1, source_target_pairs={{0,2},{1,3},{2,0},{3,1},{4,6},{5,7},{6,4},{7,5},{8,10},{9,11},{10,... | collective-permute-start | bytes 294920 | tf_op jit(solution)/shard_map/ppermute | solution.py:30
  19.9 6.9 %collective-permute-start.7 = (bf16[96,512]{1,0:T(8,128)(2,1)S(1)}, bf16[96,512]{1,0:T(8,128)(2,1)S(1)}, u32[]{:S(2)}, u32[]{:S(2)}) collective-permute-start(bf16[96,512]{1,0:T(8,128)(2,1)S(1)} %collective-permute-done.5.refs_0_), channel_id=1, source_target_pairs={{0,2},{1,3},{2,0},{3,1},{4,6},{5,7},{6,4},{7,5},{8,10},{9,11},{10,... | collective-permute-start | bytes 294920 | tf_op jit(solution)/shard_map/ppermute | solution.py:30
  22.5 6.2 %collective-permute-start.2 = (bf16[96,512]{1,0:T(8,128)(2,1)S(1)}, bf16[96,512]{1,0:T(8,128)(2,1)S(1)}, u32[]{:S(2)}, u32[]{:S(2)}) collective-permute-start(bf16[96,512]{1,0:T(8,128)(2,1)S(1)} %collective-permute-done.1.refs_0_), channel_id=1, source_target_pairs={{0,2},{1,3},{2,0},{3,1},{4,6},{5,7},{6,4},{7,5},{8,10},{9,11},{10,... | collective-permute-start | bytes 294920 | tf_op jit(solution)/shard_map/ppermute | solution.py:30
  23.1 5.7 %collective-permute-start.10 = (bf16[96,512]{1,0:T(8,128)(2,1)S(1)}, bf16[96,512]{1,0:T(8,128)(2,1)S(1)}, u32[]{:S(2)}, u32[]{:S(2)}) collective-permute-start(bf16[96,512]{1,0:T(8,128)(2,1)S(1)} %collective-permute-done.9.refs_0_), channel_id=1, source_target_pairs={{0,1},{1,0},{2,3},{3,2},{4,5},{5,4},{6,7},{7,6},{8,9},{9,8},{10,11... | collective-permute-start | bytes 294920 | tf_op jit(solution)/shard_map/ppermute | solution.py:30
  23.1 6.2 %collective-permute-start.15 = (bf16[96,512]{1,0:T(8,128)(2,1)S(1)}, bf16[96,512]{1,0:T(8,128)(2,1)S(1)}, u32[]{:S(2)}, u32[]{:S(2)}) collective-permute-start(bf16[96,512]{1,0:T(8,128)(2,1)S(1)} %collective-permute-done.14.refs_2_), channel_id=1, source_target_pairs={{0,1},{1,0},{2,3},{3,2},{4,5},{5,4},{6,7},{7,6},{8,9},{9,8},{10,11... | collective-permute-start | bytes 294920 | tf_op jit(solution)/shard_map/ppermute | solution.py:30
  24.7 7.2 %collective-permute-start.12 = (bf16[96,512]{1,0:T(8,128)(2,1)S(1)}, bf16[96,512]{1,0:T(8,128)(2,1)S(1)}, u32[]{:S(2)}, u32[]{:S(2)}) collective-permute-start(bf16[96,512]{1,0:T(8,128)(2,1)S(1)} %collective-permute-done.11.refs_2_), channel_id=1, source_target_pairs={{0,1},{1,0},{2,3},{3,2},{4,5},{5,4},{6,7},{7,6},{8,9},{9,8},{10,11... | collective-permute-start | bytes 294920 | tf_op jit(solution)/shard_map/ppermute | solution.py:30
  26.8 6.2 %collective-permute-start.6 = (bf16[96,512]{1,0:T(8,128)(2,1)S(1)}, bf16[96,512]{1,0:T(8,128)(2,1)S(1)}, u32[]{:S(2)}, u32[]{:S(2)}) collective-permute-start(bf16[96,512]{1,0:T(8,128)(2,1)S(1)} %collective-permute-done.5.refs_0_), channel_id=1, source_target_pairs={{0,1},{1,0},{2,3},{3,2},{4,5},{5,4},{6,7},{7,6},{8,9},{9,8},{10,11... | collective-permute-start | bytes 294920 | tf_op jit(solution)/shard_map/ppermute | solution.py:30
  28.7 4.3 %collective-permute-start.8 = (bf16[96,512]{1,0:T(8,128)(2,1)S(1)}, bf16[96,512]{1,0:T(8,128)(2,1)S(1)}, u32[]{:S(2)}, u32[]{:S(2)}) collective-permute-start(bf16[96,512]{1,0:T(8,128)(2,1)S(1)} %collective-permute-done.7.refs_2_), channel_id=1, source_target_pairs={{0,1},{1,0},{2,3},{3,2},{4,5},{5,4},{6,7},{7,6},{8,9},{9,8},{10,11... | collective-permute-start | bytes 294920 | tf_op jit(solution)/shard_map/ppermute | solution.py:30
  28.7 5.3 %collective-permute-start.4 = (bf16[96,512]{1,0:T(8,128)(2,1)S(1)}, bf16[96,512]{1,0:T(8,128)(2,1)S(1)}, u32[]{:S(2)}, u32[]{:S(2)}) collective-permute-start(bf16[96,512]{1,0:T(8,128)(2,1)S(1)} %collective-permute-done.1.refs_0_), channel_id=1, source_target_pairs={{0,1},{1,0},{2,3},{3,2},{4,5},{5,4},{6,7},{7,6},{8,9},{9,8},{10,11... | collective-permute-start | bytes 294920 | tf_op jit(solution)/shard_map/ppermute | solution.py:30
  29.2 5.4 %collective-permute-start.3 = (bf16[96,512]{1,0:T(8,128)(2,1)S(1)}, bf16[96,512]{1,0:T(8,128)(2,1)S(1)}, u32[]{:S(2)}, u32[]{:S(2)}) collective-permute-start(bf16[96,512]{1,0:T(8,128)(2,1)S(1)} %collective-permute-done.2.refs_0_), channel_id=1, source_target_pairs={{0,1},{1,0},{2,3},{3,2},{4,5},{5,4},{6,7},{7,6},{8,9},{9,8},{10,11... | collective-permute-start | bytes 294920 | tf_op jit(solution)/shard_map/ppermute | solution.py:30

commit v2 on v1

v2 whole, which is shorter than its diff:
```python
import functools
import math

import jax
import jax.numpy as jnp
import numpy as np
from jax import lax
from jax.experimental import pallas as pl
from jax.experimental.pallas import tpu as pltpu
from jax.sharding import PartitionSpec as P

UPCHAN = 16
TAPS = 4
GROUP = 16
PAD = 128
MIB = 1 << 20
VMEM = pl.BlockSpec(memory_space=pltpu.VMEM)
HBM = pl.BlockSpec(memory_space=pltpu.HBM)
ANY = pl.BlockSpec(memory_space=pl.ANY)


def shifted(value, axis, steps):
    count = lax.axis_size(axis)
    leading, last = (max(0, -steps), min(count, count - steps))
    return lax.ppermute(value, axis, [(source, source + steps) for source in range(leading, last)])


def swapped(value, axis, distance):
    count = lax.axis_size(axis)
    return lax.ppermute(value, axis, [(source, source ^ distance) for source in range(count)])


def dot_samples(table, samples):
    return lax.dot_general(table, samples, (((1,), (1,)), ((), ())), preferred_element_type=jnp.float32)


def window_norm():
    length = TAPS * UPCHAN
    taps = np.arange(length)
    window = np.sinc((taps - (length - 1) / 2.0) / UPCHAN)
    window = window * (0.5 - 0.5 * np.cos(2.0 * math.pi * (taps + 0.5) / length))
    return float(1.0 / np.sqrt(np.sum(window * window)))


def windows(frames, width, offset):
    length = TAPS * UPCHAN
    shape = (frames, width)
    tap = lax.broadcasted_iota(jnp.int32, shape, 1) - offset - UPCHAN * lax.broadcasted_iota(jnp.int32, shape, 0)
    place = tap.astype(jnp.float32)
    u = (place - (length - 1) / 2.0) * (math.pi / UPCHAN)
    value = jnp.sin(u) / u * (0.5 - 0.5 * jnp.cos(2.0 * math.pi * (place + 0.5) / length)) * window_norm()
    return jnp.where((tap >= 0) & (tap < length), value, 0.0)


def group_table(bins, values, offset):
    frames, width = values.shape
    sample = lax.broadcasted_iota(jnp.int32, (8, PAD), 1)
    quarter = lax.broadcasted_iota(jnp.int32, (8, PAD), 0)
    rows = []
    for k in bins:
        turn = (k * sample + 4 * (quarter - 1)) % UPCHAN
        wave = jnp.cos(turn.astype(jnp.float32) * (2.0 * math.pi / UPCHAN))
        for out in range(2):
            tiles = []
            for lane in range(0, width, PAD):
                for part in range(2):
                    quarters = out - part + 1
                    tiles.append(values[:, lane : lane + PAD] * wave[quarters : quarters + 1, :])
            rows.append(jnp.concatenate(tiles, axis=1))
    table = jnp.concatenate(rows, axis=0)
    high = table.astype(jnp.bfloat16)
    low = (table - high.astype(jnp.float32)).astype(jnp.bfloat16)
    return jnp.concatenate([high, low], axis=0)


def both_halves(table, samples, contract=1):
    total = lax.dot_general(table, samples, (((1,), (contract,)), ((), ())), preferred_element_type=jnp.float32)
    return total[: total.shape[0] // 2] + total[total.shape[0] // 2 :]


def history_kernel(bins_per_coarse, lead_width, samples_ref, tail_ref, pairs_ref):
    values = windows(8, PAD, PAD - lead_width)
    at = 0
    for coarse, bins in enumerate(bins_per_coarse):
        table = group_table(range(bins), values, PAD - lead_width)
        samples = jnp.concatenate(parts_of(samples_ref, pairs_ref, coarse, 0), axis=1)
        total = both_halves(table, samples).reshape(bins, 2, 8, -1)[:, :, :4, :]
        tail_ref[at : at + bins * 8, :] = total.reshape(bins * 8, -1)
        at += bins * 8


def parts_of(samples_ref, pairs_ref, coarse, lane):
    slots = samples_ref.shape[0]
    pairs = samples_ref[:, coarse, :, lane : lane + PAD].reshape(2 * slots, PAD)
    place = lane * 2 * slots // PAD
    pairs_ref[place : place + 2 * slots, :] = pairs.astype(jnp.float32)
    return [pairs_ref[pl.ds(place + part, slots, stride=2), :].astype(jnp.bfloat16) for part in range(2)]


def channel_kernel(plan, lead_width, volts_ref, *refs):
    spectrum_refs, early_ref, pairs_ref = refs[:-2], refs[-2], refs[-1]
    slots, _, _, width = volts_ref.shape
    frames = width // UPCHAN
    groups = frames // GROUP
    span = PAD + GROUP * UPCHAN
    me = lax.axis_index("chan")
    values = windows(GROUP, span, PAD - lead_width)
    for coarse, members in plan:
        bins = [lax.bitwise_xor(me, distance) if relative else distance for relative, distance, _ in members]
        count = len(bins)
        table = group_table(bins, values, PAD - lead_width)
        samples = [
            jnp.concatenate(parts_of(volts_ref, pairs_ref, coarse, lane), axis=1) for lane in range(0, width, PAD)
        ]
        for group in range(groups):
            total = 0.0
            for lane in range(span // PAD):
                at = group * GROUP * UPCHAN // PAD - 1 + lane
                if at >= 0:
                    columns = slice(2 * lane * PAD, 2 * (lane + 1) * PAD)
                    total = total + both_halves(table[:, columns], samples[at])
            total = total.reshape(count, 2, GROUP, slots)
            if group == 0:
                row = (coarse * UPCHAN) * 8
                early_ref[row : row + count * 8, :] = total[:, :, :4, :].reshape(count * 8, slots)
            for at, (_, _, (out, index)) in enumerate(members):
                for part in range(2):
                    row = part * frames + group * GROUP
                    spectrum_refs[out][index, row : row + GROUP, :] = total[at, part].astype(jnp.bfloat16)


def early_kernel(plan, lead_ref, early_ref, history_ref, *refs):
    spectra_in, spectra_out = refs[: len(refs) // 2], refs[len(refs) // 2 :]
    lead_width, slots = lead_ref.shape[2:]
    first = lax.axis_index("tblk") == 0
    me = lax.axis_index("chan")
    values = windows(8, PAD, PAD - lead_width)
    for coarse, members in plan:
        bins = [lax.bitwise_xor(me, distance) if relative else distance for relative, distance, _ in members]
        table = group_table(bins, values, PAD - lead_width)
        lead = []
        for part in range(2):
            lead += [jnp.zeros((PAD - lead_width, slots), jnp.bfloat16), lead_ref[part, coarse, :, :]]
        head = both_halves(table, jnp.concatenate(lead, axis=0), 0).reshape(len(bins), 2, 8, slots)[:, :, :4, :]
        head = jnp.where(first, head.reshape(len(bins) * 8, slots), 0.0)
        for at, (relative, distance, (out, index)) in enumerate(members):
            frames = spectra_in[out].shape[1] // 2
            bin_at = bins[at] + coarse * UPCHAN
            row = (coarse * UPCHAN + at) * 8
            history = history_ref[pl.ds(pl.multiple_of(bin_at * 8, 8), 8), :]
            total = early_ref[row : row + 8, :] + history + head[at * 8 : (at + 1) * 8]
            for part in range(2):
                opening = total if part == 0 else pltpu.roll(total, 4, 0)
                opening = jnp.concatenate([opening, opening], axis=0)
                old = spectra_in[out][index, part * frames : part * frames + GROUP, :].astype(jnp.float32)
                row = lax.broadcasted_iota(jnp.int32, old.shape, 0)
                new = jnp.where(row < 4, opening, old).astype(jnp.bfloat16)
                spectra_out[out][index, part * frames : part * frames + GROUP, :] = new


def choice_kernel(relative, source, slots, slot_ref, choice_ref):
    owner = lax.bitwise_xor(lax.axis_index("chan"), source) if relative else source
    for row in range(0, choice_ref.shape[0], 64):
        rows = min(64, choice_ref.shape[0] - row)
        place = lax.broadcasted_iota(jnp.int32, (rows, slot_ref.shape[1]), 0) + (owner * slots + row)
        choice_ref[row : row + rows, :] = (place == slot_ref[...]).astype(jnp.bfloat16)


def order_kernel(rows, places, fresh, choice_ref, *refs):
    pieces, new_ref = refs[: len(places)], refs[-1]
    put_in_order(rows, places, fresh, choice_ref, pieces, refs[-2], new_ref)


def put_in_order(rows, places, fresh, choice_ref, pieces, old_ref, new_ref):
    frames = rows // 2
    inputs = choice_ref.shape[1]
    stacked = [piece[at * rows : (at + 1) * rows, :] for piece, (_, at) in zip(pieces, places)]
    stacked = jnp.concatenate(stacked, axis=0)
    for column in range(0, inputs, 256):
        total = jnp.dot(stacked, choice_ref[:, column : column + 256], preferred_element_type=jnp.float32)
        total = total.astype(jnp.bfloat16)
        for at, (place, _) in enumerate(places):
            for part in range(2):
                value = total[at * rows + part * frames : at * rows + (part + 1) * frames]
                to = (slice(place * frames, (place + 1) * frames), slice(part * inputs + column, part * inputs + column + 256))
                new_ref[to] = value if fresh else old_ref[to] + value


def after(value, *others):
    return call(
        lambda *refs: None,
        jax.ShapeDtypeStruct(value.shape, value.dtype),
        value,
        *others,
        name="after",
        limit=1,
        spaces=ANY,
        outs=ANY,
        input_output_aliases={0: 0},
    )


def join_kernel(*refs):
    rows = refs[0].shape[0]
    for at, ref in enumerate(refs[:-1]):
        refs[-1][at * rows : (at + 1) * rows, :] = ref[...]


def from_other_core(parts):
    rows, slots = parts[0].shape
    if len(parts) == 1:
        return [(swapped(parts[0], "tblk", 1), 0)]
    joined = call(
        join_kernel, jax.ShapeDtypeStruct((len(parts) * rows, slots), parts[0].dtype), *parts, name="join", limit=4
    )
    other = swapped(joined, "tblk", 1)
    return [(other, at) for at in range(len(parts))]


def gram_kernel(blocks, relative, *refs):
    parts = refs[:-6]
    fine_hbm, gram_hbm, ordered, tile, result, sems = refs[-6:]
    frames = ordered.shape[0] // blocks
    width = tile.shape[0]
    own = 0 if relative else pl.multiple_of(lax.axis_index("tblk") * frames, frames)
    copies = [pltpu.make_async_copy(parts[0].at[pl.ds(own, frames), :], fine_hbm, sems.at[0])]
    copies[0].start()
    row = 0
    for part in parts:
        ordered[row : row + part.shape[0], :] = part[...]
        row += part.shape[0]
    place = pl.multiple_of(lax.axis_index("tblk") * width, width)
    tile[...] = ordered[:, pl.ds(place, width)].T
    chunk = width // 8
    for at in range(8):
        rows = slice(at * chunk, (at + 1) * chunk)
        gram = jnp.dot(tile[rows, :], ordered[...], preferred_element_type=jnp.float32)
        result[rows, :] = (gram * (1.0 / ordered.shape[0])).astype(jnp.bfloat16)
        copy = pltpu.make_async_copy(
            result.at[pl.ds(at * chunk, chunk), :], gram_hbm.at[pl.ds(at * chunk, chunk), :], sems.at[at + 1]
        )
        copy.start()
        copies.append(copy)
    for copy in copies:
        copy.wait()


def call(kernel, shapes, *operands, name, limit, spaces=VMEM, outs=VMEM, flops=0, moved=0, **options):
    spaces = spaces if isinstance(spaces, list) else [spaces] * len(operands)
    several = isinstance(shapes, list)
    return pl.pallas_call(
        kernel,
        in_specs=spaces,
        out_specs=[outs] * len(shapes) if several else outs,
        out_shape=shapes,
        compiler_params=pltpu.CompilerParams(vmem_limit_bytes=limit * MIB),
        name=name,
        cost_estimate=pl.CostEstimate(flops=flops, bytes_accessed=moved, transcendentals=0),
        **options,
    )(*operands)


def local(coarse_volts, lead_in, slot_of_input):
    slots, _, coarse, width = coarse_volts.shape
    lead_width = lead_in.shape[3]
    chans, blocks = lax.axis_size("chan"), lax.axis_size("tblk")
    frames = width // UPCHAN
    inputs = slot_of_input.shape[0]
    relative = coarse == 1 and chans == 4 and blocks == 4
    volts = coarse_volts.transpose(0, 2, 1, 3)
    lead = lead_in.transpose(1, 2, 3, 0)
    order = slot_of_input.reshape(1, inputs)

    per_coarse = [max(0, min(UPCHAN, chans - c * UPCHAN)) for c in range(coarse)]
    shape = jax.ShapeDtypeStruct

    opening = call(
        functools.partial(history_kernel, per_coarse, lead_width),
        shape((chans * 8, slots), jnp.float32),
        volts,
        name="history",
        moved=2 * MIB,
        limit=4,
        grid=(1,),
        spaces=[pl.BlockSpec((slots, coarse, 2, PAD), lambda i: (0, 0, 0, width // PAD - 1))],
        outs=pl.BlockSpec((chans * 8, slots), lambda i: (0, 0)),
        scratch_shapes=[pltpu.VMEM((2 * slots, PAD), jnp.float32)],
    )
    history = shifted(opening, "tblk", 1)

    if relative:
        plan = [(0, [(True, distance, (distance, 0)) for distance in range(chans)])]
        shapes = [shape((1, 2 * frames, slots), jnp.bfloat16)] * chans
    else:
        plan = [
            (c, [(False, k, (0, c * UPCHAN + k)) for k in range(count)]) for c, count in enumerate(per_coarse) if count
        ]
        shapes = [shape((chans, 2 * frames, slots), jnp.bfloat16)]
    *spectra, early = call(
        functools.partial(channel_kernel, plan, lead_width),
        shapes + [shape((chans * 8, slots), jnp.float32)],
        volts,
        name="channelize",
        moved=6 * MIB,
        limit=14,
        scratch_shapes=[pltpu.VMEM((2 * slots * width // PAD, PAD), jnp.float32)],
    )
    spectra = call(
        functools.partial(early_kernel, plan),
        shapes,
        lead,
        early,
        history,
        *spectra,
        name="early",
        limit=2,
        input_output_aliases={3 + at: at for at in range(len(shapes))},
    )

    sources = range(chans) if relative else [0]
    wide = slots if relative else inputs
    choices = [
        call(
            functools.partial(choice_kernel, relative, source, wide),
            shape((wide, inputs), jnp.bfloat16),
            order,
            name="choice",
            moved=2 * wide * inputs,
            limit=2 if relative else 10,
        )
        for source in sources
    ]
    mine = blocks // 2 if relative else blocks
    ordered_shape = shape((mine * frames, 2 * inputs), jnp.bfloat16)

    def put(source, given, ordered):
        given = [(to, *piece) for to, piece in given]
        old = [] if ordered is None else [ordered]
        return call(
            functools.partial(order_kernel, 2 * frames, [(to, at) for to, _, at in given], ordered is None),
            ordered_shape,
            choices[source],
            *[array for _, array, _ in given],
            *old,
            name="order",
            flops=4 * len(given) * frames * wide * inputs,
            limit=6 if relative else 24,
            input_output_aliases={1 + len(given): 0} if old else {},
        )

    if relative:
        spectra = [s[0] for s in spectra]
        own, one = spectra[0], spectra[1]
        z2, z3 = swapped(spectra[2], "chan", 2), swapped(spectra[3], "chan", 3)
        z1 = swapped(one, "chan", 1)
        x1 = lax.ppermute(
            one,
            ("chan", "tblk"),
            [(c * blocks + b, (c ^ 1) * blocks + (b ^ 2)) for c in range(chans) for b in range(blocks)],
        )
        x0 = swapped(own, "tblk", 2)
        x3 = swapped(z3, "tblk", 2)
        x2 = swapped(z2, "tblk", 2)
        ordered = put(0, [(0, (own, 0)), (1, (x0, 0))], None)
        ordered = put(1, [(0, (z1, 0)), (1, (x1, 0))], ordered)
        ordered = put(3, [(0, (z3, 0)), (1, (x3, 0))], ordered)
        ordered = put(2, [(0, (z2, 0)), (1, (x2, 0))], ordered)
        halves = [ordered, swapped(ordered, "tblk", 1)]
    else:
        owned = lax.all_to_all(spectra[0], "chan", split_axis=0, concat_axis=2, tiled=True)[0]
        all_time = lax.all_gather(owned, "tblk", axis=0)
        halves = [put(0, [(b, (all_time[b], 0)) for b in range(blocks)], None)]

    tile_rows = 2 * inputs // blocks
    fine, gram = call(
        functools.partial(gram_kernel, blocks, relative),
        [shape((frames, 2 * inputs), jnp.bfloat16), shape((tile_rows, 2 * inputs), jnp.bfloat16)],
        *halves,
        name="gram",
        moved=12 * MIB,
        limit=20 if relative else 40,
        outs=HBM,
        scratch_shapes=[
            pltpu.VMEM((blocks * frames, 2 * inputs), jnp.bfloat16),
            pltpu.VMEM((tile_rows, blocks * frames), jnp.bfloat16),
            pltpu.VMEM((tile_rows, 2 * inputs), jnp.bfloat16),
            pltpu.SemaphoreType.DMA((9,)),
        ],
    )
    return fine[None], gram[None]


def solution(mesh):
    placed = (P("chan", None, "grp", "tblk"), P("chan", None, "grp", None), P())
    return jax.shard_map(
        local,
        mesh=mesh,
        in_specs=placed,
        out_specs=(P(("grp", "chan"), "tblk", None), P(("grp", "chan"), "tblk", None)),
        check_vma=False,
    )
```

time: 39.4 us -> 33 us (0.84)
  waiting for transfers between devices: 8.88 us -> 5.58 us
  local copies, waits for them, and re-layouts: 4.21 us -> 1.41 us
  Pallas kernels: 12.2 us -> 10.5 us
  starting transfers between devices: 13 us -> 14.6 us
    ppermute x15 -> x7, waiting for transfers between devices: 8.88 us -> 5.24 us  [swapped(): lax.ppermute(value, axis, [(source, source ^ distance) for source in rang...]
    unnamed x14 -> x8, local copies, waits for them, and re-layouts: 4.05 us -> 1.41 us
    pallas_call x12, Pallas kernels: 12.2 us -> 10.5 us  [call(): pl.pallas_call(kernel, in_specs=spaces, out_specs=[outs] * len(shapes) if...]
    ppermute x15 -> x7, starting transfers between devices: 10.6 us -> 12 us  [swapped(): lax.ppermute(value, axis, [(source, source ^ distance) for source in rang...]
  transfers between devices with their start and end apart: 16 -> 9, of which waited for: 5 -> 5; matrix products, arithmetic and copies ran while one was open for 0% -> 0% of each run, Pallas kernels for 18% -> 16%
where the time goes in v2:
time: 33 us; the launch traced here: 32.9 us
  starting transfers between devices  14.6 us (44%)
  Pallas kernels  10.5 us (32%)
  waiting for transfers between devices  5.58 us (17%)
  local copies, waits for them, and re-layouts  1.41 us (4%)
  between operations  0.77 us (2%)
    ppermute x7, starting transfers between devices, swapped(): lax.ppermute(value, axis, [(source, source ^ distance) for source in rang...  12 us
    pallas_call x12, Pallas kernels, call(): pl.pallas_call(kernel, in_specs=spaces, out_specs=[outs] * len(shapes) if...  10.5 us
    ppermute x7, waiting for transfers between devices, swapped(): lax.ppermute(value, axis, [(source, source ^ distance) for source in rang...  5.24 us
    ppermute x1, starting transfers between devices, shifted(): lax.ppermute(value, axis, [(source, source + steps) for source in range(l...  2.36 us
    unnamed x8, local copies, waits for them, and re-layouts  1.41 us
  transfers between devices with their start and end apart: 9, of which 5 were waited for; matrix products, arithmetic and copies ran while one was open for 0% of the time, Pallas kernels for 16%

profile of v2, /device:TPU:0, one launch (start us, length us, event | category | flops | bytes accessed | tf_op | source)
XLA Modules:
  0.0 32.9 jit_solution(12198729064020097328)
XLA Ops:
  0.6 1.4 %copy-done = bf16[512,2,1,768]{3,1,2,0:T(2,128)(2,1)S(1)} copy-done((bf16[512,2,1,768]{3,1,2,0:T(2,128)(2,1)S(1)}, bf16[512,2,1,768]{3,1,2,0:T(2,128)(2,1)}, u32[]{:S(2)}) %copy-start) | copy-done | bytes 1572888
  2.0 0.6 %history.1 = f32[32,512]{1,0:T(8,128)S(1)} custom-call(bf16[512,1,2,768]{3,2,1,0:T(2,128)(2,1)S(1)} %bitcast.9), custom_call_target="tpu_custom_call" | custom-call | bytes 2097152 | tf_op jit(solution)/shard_map/history/pallas_call | solution.py:251
  2.6 2.4 %collective-permute-start = (f32[32,512]{1,0:T(8,128)S(1)}, f32[32,512]{1,0:T(8,128)S(1)}, u32[]{:S(2)}, u32[]{:S(2)}) collective-permute-start(f32[32,512]{1,0:T(8,128)S(1)} %history.1), channel_id=1, source_target_pairs={{0,1},{1,2},{2,3},{4,5},{5,6},{6,7},{8,9},{9,10},{10,11},{12,13},{... | collective-permute-start | bytes 196616 | tf_op jit(solution)/shard_map/ppermute | solution.py:25
  5.0 0.0 copy-done.1
  5.0 1.9 %channelize.1 = (bf16[1,96,512]{2,1,0:T(8,128)(2,1)S(1)}, bf16[1,96,512]{2,1,0:T(8,128)(2,1)S(1)}, bf16[1,96,512]{2,1,0:T(8,128)(2,1)S(1)}, bf16[1,96,512]{2,1,0:T(8,128)(2,1)S(1)}, f32[32,512]{1,0:T(8,128)S(1)}) custom-call(bf16[512,1,2,768]{3,2,1,0:T(2,128)(2,1)S(1)} %bitcast.10), custom_call_target="tpu_custom_call" | custom-call | bytes 6291456 | tf_op jit(solution)/shard_map/channelize/pallas_call | solution.py:251
  6.9 0.0 collective-permute-done.history_ref
  6.9 0.3 early.1
  7.2 4.5 %collective-permute-start.3 = (bf16[96,512]{1,0:T(8,128)(2,1)S(1)}, bf16[96,512]{1,0:T(8,128)(2,1)S(1)}, u32[]{:S(2)}, u32[]{:S(2)}) collective-permute-start(bf16[96,512]{1,0:T(8,128)(2,1)S(1)} %bitcast.21), channel_id=1, source_target_pairs={{0,12},{4,8},{8,4},{12,0},{1,13},{5,9},{9,5},{13,1},{2,14},{6,10},... | collective-permute-start | bytes 294920 | tf_op jit(solution)/shard_map/ppermute | solution.py:30
  11.7 0.0 collective-permute-start.1
  11.7 3.4 %collective-permute-start.7 = (bf16[96,512]{1,0:T(8,128)(2,1)S(1)}, bf16[96,512]{1,0:T(8,128)(2,1)S(1)}, u32[]{:S(2)}, u32[]{:S(2)}) collective-permute-start(bf16[96,512]{1,0:T(8,128)(2,1)S(1)} %bitcast.11), channel_id=1, source_target_pairs={{0,2},{1,3},{2,0},{3,1},{4,6},{5,7},{6,4},{7,5},{8,10},{9,11},{10,... | collective-permute-start | bytes 294920 | tf_op jit(solution)/shard_map/ppermute | solution.py:30
  15.1 0.2 collective-permute-start.6
  15.3 1.2 %collective-permute-start.5 = (bf16[96,512]{1,0:T(8,128)(2,1)S(1)}, bf16[96,512]{1,0:T(8,128)(2,1)S(1)}, u32[]{:S(2)}, u32[]{:S(2)}) collective-permute-start(bf16[96,512]{1,0:T(8,128)(2,1)S(1)} %bitcast.19), channel_id=1, source_target_pairs={{0,4},{4,0},{8,12},{12,8},{1,5},{5,1},{9,13},{13,9},{2,6},{6,2},{1... | collective-permute-start | bytes 294920 | tf_op jit(solution)/shard_map/ppermute | solution.py:30
  16.6 0.0 collective-permute-done.3.refs_0_
  16.6 2.0 %collective-permute-start.4 = (bf16[96,512]{1,0:T(8,128)(2,1)S(1)}, bf16[96,512]{1,0:T(8,128)(2,1)S(1)}, u32[]{:S(2)}, u32[]{:S(2)}) collective-permute-start(bf16[96,512]{1,0:T(8,128)(2,1)S(1)} %collective-permute-done.3.refs_0_), channel_id=1, source_target_pairs={{0,2},{1,3},{2,0},{3,1},{4,6},{5,7},{6,4},{7,5},{8,10},{9,11},{10,... | collective-permute-start | bytes 294920 | tf_op jit(solution)/shard_map/ppermute | solution.py:30
  18.6 0.4 %choice.7.choice_ref = bf16[512,2048]{1,0:T(8,128)(2,1)S(1)} custom-call(s32[1,2048]{1,0:T(1,128)S(1)} %bitcast.13), custom_call_target="tpu_custom_call" | custom-call | bytes 2097152 | tf_op jit(solution)/shard_map/choice/pallas_call | solution.py:251
  18.9 0.4 %choice.6.choice_ref = bf16[512,2048]{1,0:T(8,128)(2,1)S(1)} custom-call(s32[1,2048]{1,0:T(1,128)S(1)} %bitcast.14), custom_call_target="tpu_custom_call" | custom-call | bytes 2097152 | tf_op jit(solution)/shard_map/choice/pallas_call | solution.py:251
  19.3 0.4 %choice.5.choice_ref = bf16[512,2048]{1,0:T(8,128)(2,1)S(1)} custom-call(s32[1,2048]{1,0:T(1,128)S(1)} %bitcast.15), custom_call_target="tpu_custom_call" | custom-call | bytes 2097152 | tf_op jit(solution)/shard_map/choice/pallas_call | solution.py:251
  19.7 0.4 %choice.4.choice_ref = bf16[512,2048]{1,0:T(8,128)(2,1)S(1)} custom-call(s32[1,2048]{1,0:T(1,128)S(1)} %bitcast.16), custom_call_target="tpu_custom_call" | custom-call | bytes 2097152 | tf_op jit(solution)/shard_map/choice/pallas_call | solution.py:251
  20.1 0.5 %collective-permute-done.1.refs_0_ = bf16[96,512]{1,0:T(8,128)(2,1)S(1)} collective-permute-done((bf16[96,512]{1,0:T(8,128)(2,1)S(1)}, bf16[96,512]{1,0:T(8,128)(2,1)S(1)}, u32[]{:S(2)}, u32[]{:S(2)}) %collective-permute-start.1) | collective-permute-done | bytes 98336 | tf_op jit(solution)/shard_map/ppermute | solution.py:30
  20.5 0.7 %collective-permute-start.2 = (bf16[96,512]{1,0:T(8,128)(2,1)S(1)}, bf16[96,512]{1,0:T(8,128)(2,1)S(1)}, u32[]{:S(2)}, u32[]{:S(2)}) collective-permute-start(bf16[96,512]{1,0:T(8,128)(2,1)S(1)} %collective-permute-done.1.refs_0_), channel_id=1, source_target_pairs={{0,2},{1,3},{2,0},{3,1},{4,6},{5,7},{6,4},{7,5},{8,10},{9,11},{10,... | collective-permute-start | bytes 294920 | tf_op jit(solution)/shard_map/ppermute | solution.py:30
  21.3 0.0 collective-permute-done.7.refs_1_
  21.3 0.6 %order.4.refs_2_ = bf16[96,4096]{1,0:T(8,128)(2,1)S(1)} custom-call(bf16[512,2048]{1,0:T(8,128)(2,1)S(1)} %choice.7.choice_ref, bf16[96,512]{1,0:T(8,128)(2,1)S(1)} %bitcast.12, bf16[96,512]{1,0:T(8,128)(2,1)S(1)} %collective-permute-done.7.refs_1_), custom_call_target="tpu_custom_call" | custom-call | flops 402653184 | tf_op jit(solution)/shard_map/order/pallas_call | solution.py:251
  21.9 0.3 %collective-permute-done.6.refs_1_ = bf16[96,512]{1,0:T(8,128)(2,1)S(1)} collective-permute-done((bf16[96,512]{1,0:T(8,128)(2,1)S(1)}, bf16[96,512]{1,0:T(8,128)(2,1)S(1)}, u32[]{:S(2)}, u32[]{:S(2)}) %collective-permute-start.6) | collective-permute-done | bytes 98336 | tf_op jit(solution)/shard_map/ppermute | solution.py:356
  22.2 1.0 %collective-permute-done.5.refs_0_ = bf16[96,512]{1,0:T(8,128)(2,1)S(1)} collective-permute-done((bf16[96,512]{1,0:T(8,128)(2,1)S(1)}, bf16[96,512]{1,0:T(8,128)(2,1)S(1)}, u32[]{:S(2)}, u32[]{:S(2)}) %collective-permute-start.5) | collective-permute-done | bytes 98336 | tf_op jit(solution)/shard_map/ppermute | solution.py:30
  23.3 0.6 %order.5.refs_2_ = bf16[96,4096]{1,0:T(8,128)(2,1)S(1)} custom-call(bf16[512,2048]{1,0:T(8,128)(2,1)S(1)} %choice.6.choice_ref, bf16[96,512]{1,0:T(8,128)(2,1)S(1)} %collective-permute-done.5.refs_0_, bf16[96,512]{1,0:T(8,128)(2,1)S(1)} %collective-permute-done.6.refs_1_, bf16[96,4096]{1,0:T(8,128)(2,1)S(1)} %order.4.refs_2_), custom_call_target="tpu_custom_call", output_to_operand_aliasing={{}: (3, {})} | custom-call | flops 402653184 | tf_op jit(solution)/shard_map/order/pallas_call | solution.py:251
  23.9 0.0 collective-permute-done.4.refs_1_
  23.9 0.6 %order.6.refs_2_ = bf16[96,4096]{1,0:T(8,128)(2,1)S(1)} custom-call(bf16[512,2048]{1,0:T(8,128)(2,1)S(1)} %choice.5.choice_ref, bf16[96,512]{1,0:T(8,128)(2,1)S(1)} %collective-permute-done.3.refs_0_, bf16[96,512]{1,0:T(8,128)(2,1)S(1)} %collective-permute-done.4.refs_1_, bf16[96,4096]{1,0:T(8,128)(2,1)S(1)} %order.5.refs_2_), custom_call_target="tpu_custom_call", output_to_operand_aliasing={{}: (3, {})} | custom-call | flops 402653184 | tf_op jit(solution)/shard_map/order/pallas_call | solution.py:251
  24.5 1.4 %collective-permute-done.2.refs_1_ = bf16[96,512]{1,0:T(8,128)(2,1)S(1)} collective-permute-done((bf16[96,512]{1,0:T(8,128)(2,1)S(1)}, bf16[96,512]{1,0:T(8,128)(2,1)S(1)}, u32[]{:S(2)}, u32[]{:S(2)}) %collective-permute-start.2) | collective-permute-done | bytes 98336 | tf_op jit(solution)/shard_map/ppermute | solution.py:30
  25.9 0.6 %order.7.refs_0_ = bf16[96,4096]{1,0:T(8,128)(2,1)S(1)} custom-call(bf16[512,2048]{1,0:T(8,128)(2,1)S(1)} %choice.4.choice_ref, bf16[96,512]{1,0:T(8,128)(2,1)S(1)} %collective-permute-done.1.refs_0_, bf16[96,512]{1,0:T(8,128)(2,1)S(1)} %collective-permute-done.2.refs_1_, bf16[96,4096]{1,0:T(8,128)(2,1)S(1)} %order.6.refs_2_), custom_call_target="tpu_custom_call", output_to_operand_aliasing={{}: (3, {})} | custom-call | flops 402653184 | tf_op jit(solution)/shard_map/order/pallas_call | solution.py:251
  26.5 0.1 collective-permute-start.8
  26.6 2.3 %collective-permute-done.8.refs_1_ = bf16[96,4096]{1,0:T(8,128)(2,1)S(1)} collective-permute-done((bf16[96,4096]{1,0:T(8,128)(2,1)S(1)}, bf16[96,4096]{1,0:T(8,128)(2,1)S(1)}, u32[]{:S(2)}, u32[]{:S(2)}) %collective-permute-start.8) | collective-permute-done | bytes 786464 | tf_op jit(solution)/shard_map/ppermute | solution.py:30
  28.9 4.0 %gram.1 = (bf16[48,4096]{1,0:T(8,128)(2,1)}, bf16[1024,4096]{1,0:T(8,128)(2,1)}) custom-call(bf16[96,4096]{1,0:T(8,128)(2,1)S(1)} %order.7.refs_0_, bf16[96,4096]{1,0:T(8,128)(2,1)S(1)} %collective-permute-done.8.refs_1_), custom_call_target="tpu_custom_call" | custom-call | bytes 12582912 | tf_op jit(solution)/shard_map/gram/pallas_call | solution.py:251
  (6 shorter events, 0.0 us)
Async XLA Ops:
  0.6 1.4 %copy-start = (bf16[512,2,1,768]{3,1,2,0:T(2,128)(2,1)S(1)}, bf16[512,2,1,768]{3,1,2,0:T(2,128)(2,1)}, u32[]{:S(2)}) copy-start(bf16[512,2,1,768]{3,1,2,0:T(2,128)(2,1)} %param.3) | copy-start | bytes 4718596
  2.0 2.9 %copy-start.1 = (bf16[512,2,1,768]{3,1,2,0:T(2,128)(2,1)S(1)}, bf16[512,2,1,768]{3,1,2,0:T(2,128)(2,1)}, u32[]{:S(2)}) copy-start(bf16[512,2,1,768]{3,1,2,0:T(2,128)(2,1)} %param.3) | copy-start | bytes 4718596
  2.0 4.8 %copy-start.3 = (bf16[512,2,1,48]{0,3,2,1:T(8,128)(2,1)S(1)}, bf16[512,2,1,48]{0,3,2,1:T(8,128)(2,1)}, u32[]{:S(2)}) copy-start(bf16[512,2,1,48]{0,3,2,1:T(8,128)(2,1)} %param.4) | copy-start | bytes 294916
  2.0 16.5 %copy-start.2 = (s32[2048]{0:T(1024)S(1)}, s32[2048]{0:T(1024)}, u32[]{:S(2)}) copy-start(s32[2048]{0:T(1024)} %param.5) | copy-start | bytes 24580
  2.6 4.3 %collective-permute-start = (f32[32,512]{1,0:T(8,128)S(1)}, f32[32,512]{1,0:T(8,128)S(1)}, u32[]{:S(2)}, u32[]{:S(2)}) collective-permute-start(f32[32,512]{1,0:T(8,128)S(1)} %history.1), channel_id=1, source_target_pairs={{0,1},{1,2},{2,3},{4,5},{5,6},{6,7},{8,9},{9,10},{10,11},{12,13},{... | collective-permute-start | bytes 196616 | tf_op jit(solution)/shard_map/ppermute | solution.py:25
  7.2 9.4 %collective-permute-start.3 = (bf16[96,512]{1,0:T(8,128)(2,1)S(1)}, bf16[96,512]{1,0:T(8,128)(2,1)S(1)}, u32[]{:S(2)}, u32[]{:S(2)}) collective-permute-start(bf16[96,512]{1,0:T(8,128)(2,1)S(1)} %bitcast.21), channel_id=1, source_target_pairs={{0,12},{4,8},{8,4},{12,0},{1,13},{5,9},{9,5},{13,1},{2,14},{6,10},... | collective-permute-start | bytes 294920 | tf_op jit(solution)/shard_map/ppermute | solution.py:30
  11.7 8.9 %collective-permute-start.1 = (bf16[96,512]{1,0:T(8,128)(2,1)S(1)}, bf16[96,512]{1,0:T(8,128)(2,1)S(1)}, u32[]{:S(2)}, u32[]{:S(2)}) collective-permute-start(bf16[96,512]{1,0:T(8,128)(2,1)S(1)} %bitcast.20), channel_id=1, source_target_pairs={{0,8},{4,12},{8,0},{12,4},{1,9},{5,13},{9,1},{13,5},{2,10},{6,14},... | collective-permute-start | bytes 294920 | tf_op jit(solution)/shard_map/ppermute | solution.py:30
  11.7 9.6 %collective-permute-start.7 = (bf16[96,512]{1,0:T(8,128)(2,1)S(1)}, bf16[96,512]{1,0:T(8,128)(2,1)S(1)}, u32[]{:S(2)}, u32[]{:S(2)}) collective-permute-start(bf16[96,512]{1,0:T(8,128)(2,1)S(1)} %bitcast.11), channel_id=1, source_target_pairs={{0,2},{1,3},{2,0},{3,1},{4,6},{5,7},{6,4},{7,5},{8,10},{9,11},{10,... | collective-permute-start | bytes 294920 | tf_op jit(solution)/shard_map/ppermute | solution.py:30
  15.1 7.1 %collective-permute-start.6 = (bf16[96,512]{1,0:T(8,128)(2,1)S(1)}, bf16[96,512]{1,0:T(8,128)(2,1)S(1)}, u32[]{:S(2)}, u32[]{:S(2)}) collective-permute-start(bf16[96,512]{1,0:T(8,128)(2,1)S(1)} %bitcast.18), channel_id=1, source_target_pairs={{0,6},{1,7},{2,4},{3,5},{4,2},{5,3},{6,0},{7,1},{8,14},{9,15},{10,... | collective-permute-start | bytes 294920 | tf_op jit(solution)/shard_map/ppermute | solution.py:356
  15.3 7.9 %collective-permute-start.5 = (bf16[96,512]{1,0:T(8,128)(2,1)S(1)}, bf16[96,512]{1,0:T(8,128)(2,1)S(1)}, u32[]{:S(2)}, u32[]{:S(2)}) collective-permute-start(bf16[96,512]{1,0:T(8,128)(2,1)S(1)} %bitcast.19), channel_id=1, source_target_pairs={{0,4},{4,0},{8,12},{12,8},{1,5},{5,1},{9,13},{13,9},{2,6},{6,2},{1... | collective-permute-start | bytes 294920 | tf_op jit(solution)/shard_map/ppermute | solution.py:30
  16.6 7.3 %collective-permute-start.4 = (bf16[96,512]{1,0:T(8,128)(2,1)S(1)}, bf16[96,512]{1,0:T(8,128)(2,1)S(1)}, u32[]{:S(2)}, u32[]{:S(2)}) collective-permute-start(bf16[96,512]{1,0:T(8,128)(2,1)S(1)} %collective-permute-done.3.refs_0_), channel_id=1, source_target_pairs={{0,2},{1,3},{2,0},{3,1},{4,6},{5,7},{6,4},{7,5},{8,10},{9,11},{10,... | collective-permute-start | bytes 294920 | tf_op jit(solution)/shard_map/ppermute | solution.py:30
  20.5 5.4 %collective-permute-start.2 = (bf16[96,512]{1,0:T(8,128)(2,1)S(1)}, bf16[96,512]{1,0:T(8,128)(2,1)S(1)}, u32[]{:S(2)}, u32[]{:S(2)}) collective-permute-start(bf16[96,512]{1,0:T(8,128)(2,1)S(1)} %collective-permute-done.1.refs_0_), channel_id=1, source_target_pairs={{0,2},{1,3},{2,0},{3,1},{4,6},{5,7},{6,4},{7,5},{8,10},{9,11},{10,... | collective-permute-start | bytes 294920 | tf_op jit(solution)/shard_map/ppermute | solution.py:30
  26.5 2.4 %collective-permute-start.8 = (bf16[96,4096]{1,0:T(8,128)(2,1)S(1)}, bf16[96,4096]{1,0:T(8,128)(2,1)S(1)}, u32[]{:S(2)}, u32[]{:S(2)}) collective-permute-start(bf16[96,4096]{1,0:T(8,128)(2,1)S(1)} %order.7.refs_0_), channel_id=1, source_target_pairs={{0,1},{1,0},{2,3},{3,2},{4,5},{5,4},{6,7},{7,6},{8,9},{9,8},{10,11... | collective-permute-start | bytes 2359304 | tf_op jit(solution)/shard_map/ppermute | solution.py:30

commit v3 on v2

--- a/solution.py
+++ b/solution.py
@@ -78,21 +78,22 @@
     return total[: total.shape[0] // 2] + total[total.shape[0] // 2 :]
 
 
-def history_kernel(bins_per_coarse, lead_width, samples_ref, tail_ref, pairs_ref):
+def history_kernel(bins_per_coarse, lead_width, volts_ref, tail_ref, pairs_ref):
+    width = volts_ref.shape[3]
     values = windows(8, PAD, PAD - lead_width)
     at = 0
     for coarse, bins in enumerate(bins_per_coarse):
         table = group_table(range(bins), values, PAD - lead_width)
-        samples = jnp.concatenate(parts_of(samples_ref, pairs_ref, coarse, 0), axis=1)
+        samples = jnp.concatenate(parts_of(volts_ref, pairs_ref, coarse, width - PAD, 0), axis=1)
         total = both_halves(table, samples).reshape(bins, 2, 8, -1)[:, :, :4, :]
         tail_ref[at : at + bins * 8, :] = total.reshape(bins * 8, -1)
         at += bins * 8
 
 
-def parts_of(samples_ref, pairs_ref, coarse, lane):
+def parts_of(samples_ref, pairs_ref, coarse, lane, place=None):
     slots = samples_ref.shape[0]
     pairs = samples_ref[:, coarse, :, lane : lane + PAD].reshape(2 * slots, PAD)
-    place = lane * 2 * slots // PAD
+    place = lane * 2 * slots // PAD if place is None else place
     pairs_ref[place : place + 2 * slots, :] = pairs.astype(jnp.float32)
     return [pairs_ref[pl.ds(place + part, slots, stride=2), :].astype(jnp.bfloat16) for part in range(2)]
 
@@ -130,25 +131,34 @@
 
 
 def early_kernel(plan, lead_ref, early_ref, history_ref, *refs):
+    head_ref, refs = refs[-1], refs[:-1]
     spectra_in, spectra_out = refs[: len(refs) // 2], refs[len(refs) // 2 :]
     lead_width, slots = lead_ref.shape[2:]
     first = lax.axis_index("tblk") == 0
     me = lax.axis_index("chan")
-    values = windows(8, PAD, PAD - lead_width)
+    head_ref[...] = jnp.zeros_like(head_ref)
+
+    @pl.when(first)
+    def _():
+        values = windows(8, PAD, PAD - lead_width)
+        for coarse, members in plan:
+            bins = [lax.bitwise_xor(me, distance) if relative else distance for relative, distance, _ in members]
+            table = group_table(bins, values, PAD - lead_width)
+            lead = []
+            for part in range(2):
+                lead += [jnp.zeros((PAD - lead_width, slots), jnp.bfloat16), lead_ref[part, coarse, :, :]]
+            head = both_halves(table, jnp.concatenate(lead, axis=0), 0).reshape(len(bins), 2, 8, slots)[:, :, :4, :]
+            row = coarse * UPCHAN * 8
+            head_ref[row : row + len(bins) * 8, :] = head.reshape(len(bins) * 8, slots)
+
     for coarse, members in plan:
         bins = [lax.bitwise_xor(me, distance) if relative else distance for relative, distance, _ in members]
-        table = group_table(bins, values, PAD - lead_width)
-        lead = []
-        for part in range(2):
-            lead += [jnp.zeros((PAD - lead_width, slots), jnp.bfloat16), lead_ref[part, coarse, :, :]]
-        head = both_halves(table, jnp.concatenate(lead, axis=0), 0).reshape(len(bins), 2, 8, slots)[:, :, :4, :]
-        head = jnp.where(first, head.reshape(len(bins) * 8, slots), 0.0)
         for at, (relative, distance, (out, index)) in enumerate(members):
             frames = spectra_in[out].shape[1] // 2
             bin_at = bins[at] + coarse * UPCHAN
             row = (coarse * UPCHAN + at) * 8
             history = history_ref[pl.ds(pl.multiple_of(bin_at * 8, 8), 8), :]
-            total = early_ref[row : row + 8, :] + history + head[at * 8 : (at + 1) * 8]
+            total = early_ref[row : row + 8, :] + history + head_ref[row : row + 8, :]
             for part in range(2):
                 opening = total if part == 0 else pltpu.roll(total, 4, 0)
                 opening = jnp.concatenate([opening, opening], axis=0)
@@ -281,9 +291,6 @@
         name="history",
         moved=2 * MIB,
         limit=4,
-        grid=(1,),
-        spaces=[pl.BlockSpec((slots, coarse, 2, PAD), lambda i: (0, 0, 0, width // PAD - 1))],
-        outs=pl.BlockSpec((chans * 8, slots), lambda i: (0, 0)),
         scratch_shapes=[pltpu.VMEM((2 * slots, PAD), jnp.float32)],
     )
     history = shifted(opening, "tblk", 1)
@@ -314,6 +321,7 @@
         *spectra,
         name="early",
         limit=2,
+        scratch_shapes=[pltpu.VMEM((chans * 8, slots), jnp.float32)],
         input_output_aliases={3 + at: at for at in range(len(shapes))},
     )
 
@@ -325,7 +333,7 @@
             shape((wide, inputs), jnp.bfloat16),
             order,
             name="choice",
-            moved=2 * wide * inputs,
+            moved=0,
             limit=2 if relative else 10,
         )
         for source in sources
@@ -361,10 +369,10 @@
         x0 = swapped(own, "tblk", 2)
         x3 = swapped(z3, "tblk", 2)
         x2 = swapped(z2, "tblk", 2)
-        ordered = put(0, [(0, (own, 0)), (1, (x0, 0))], None)
-        ordered = put(1, [(0, (z1, 0)), (1, (x1, 0))], ordered)
+        ordered = put(1, [(0, (z1, 0)), (1, (x1, 0))], None)
+        ordered = put(0, [(0, (own, 0)), (1, (x0, 0))], ordered)
+        ordered = put(2, [(0, (z2, 0)), (1, (x2, 0))], ordered)
         ordered = put(3, [(0, (z3, 0)), (1, (x3, 0))], ordered)
-        ordered = put(2, [(0, (z2, 0)), (1, (x2, 0))], ordered)
         halves = [ordered, swapped(ordered, "tblk", 1)]
     else:
         owned = lax.all_to_all(spectra[0], "chan", split_axis=0, concat_axis=2, tiled=True)[0]

time: 33 us -> 32.8 us (level)
  waiting for transfers between devices: 5.58 us -> 4.8 us
  starting transfers between devices: 14.6 us -> 15.2 us
    ppermute x1, starting transfers between devices: 0.22 us -> 2.83 us  [local(): lax.ppermute(one, ('chan', 'tblk'), [(c * blocks + b, (c ^ 1) * blocks +...]
    ppermute x7, starting transfers between devices: 12 us -> 9.87 us  [swapped(): lax.ppermute(value, axis, [(source, source ^ distance) for source in rang...]
    ppermute x7, waiting for transfers between devices: 5.24 us -> 4.8 us  [swapped(): lax.ppermute(value, axis, [(source, source ^ distance) for source in rang...]
  transfers between devices with their start and end apart: 9 -> 9, of which waited for: 5 -> 4; matrix products, arithmetic and copies ran while one was open for 0% -> 0% of each run, Pallas kernels for 16% -> 16%
where the time goes in v3:
time: 32.8 us; the launch traced here: 32.6 us
  starting transfers between devices  15.2 us (46%)
  Pallas kernels  10.4 us (32%)
  waiting for transfers between devices  4.8 us (15%)
  local copies, waits for them, and re-layouts  1.41 us (4%)
  between operations  0.78 us (2%)
    pallas_call x12, Pallas kernels, call(): pl.pallas_call(kernel, in_specs=spaces, out_specs=[outs] * len(shapes) if...  10.4 us
    ppermute x7, starting transfers between devices, swapped(): lax.ppermute(value, axis, [(source, source ^ distance) for source in rang...  9.87 us
    ppermute x7, waiting for transfers between devices, swapped(): lax.ppermute(value, axis, [(source, source ^ distance) for source in rang...  4.8 us
    ppermute x1, starting transfers between devices, local(): lax.ppermute(one, ('chan', 'tblk'), [(c * blocks + b, (c ^ 1) * blocks +...  2.83 us
    ppermute x1, starting transfers between devices, shifted(): lax.ppermute(value, axis, [(source, source + steps) for source in range(l...  2.49 us
    unnamed x8, local copies, waits for them, and re-layouts  1.41 us
  transfers between devices with their start and end apart: 9, of which 4 were waited for; matrix products, arithmetic and copies ran while one was open for 0% of the time, Pallas kernels for 16%

profile of v3, /device:TPU:0, one launch (start us, length us, event | category | flops | bytes accessed | tf_op | source)
XLA Modules:
  0.0 32.6 jit_solution(12578883140952790443)
XLA Ops:
  0.6 0.0 copy-start
  0.6 1.4 %copy-done = bf16[512,2,1,768]{3,1,2,0:T(2,128)(2,1)S(1)} copy-done((bf16[512,2,1,768]{3,1,2,0:T(2,128)(2,1)S(1)}, bf16[512,2,1,768]{3,1,2,0:T(2,128)(2,1)}, u32[]{:S(2)}) %copy-start) | copy-done | bytes 1572888
  2.0 0.5 %history.1 = f32[32,512]{1,0:T(8,128)S(1)} custom-call(bf16[512,1,2,768]{3,2,1,0:T(2,128)(2,1)S(1)} %bitcast.9), custom_call_target="tpu_custom_call" | custom-call | bytes 2097152 | tf_op jit(solution)/shard_map/history/pallas_call | solution.py:261
  2.5 2.5 %collective-permute-start = (f32[32,512]{1,0:T(8,128)S(1)}, f32[32,512]{1,0:T(8,128)S(1)}, u32[]{:S(2)}, u32[]{:S(2)}) collective-permute-start(f32[32,512]{1,0:T(8,128)S(1)} %history.1), channel_id=1, source_target_pairs={{0,1},{1,2},{2,3},{4,5},{5,6},{6,7},{8,9},{9,10},{10,11},{12,13},{... | collective-permute-start | bytes 196616 | tf_op jit(solution)/shard_map/ppermute | solution.py:25
  5.0 1.9 %channelize.1 = (bf16[1,96,512]{2,1,0:T(8,128)(2,1)S(1)}, bf16[1,96,512]{2,1,0:T(8,128)(2,1)S(1)}, bf16[1,96,512]{2,1,0:T(8,128)(2,1)S(1)}, bf16[1,96,512]{2,1,0:T(8,128)(2,1)S(1)}, f32[32,512]{1,0:T(8,128)S(1)}) custom-call(bf16[512,1,2,768]{3,2,1,0:T(2,128)(2,1)S(1)} %bitcast.10), custom_call_target="tpu_custom_call" | custom-call | bytes 6291456 | tf_op jit(solution)/shard_map/channelize/pallas_call | solution.py:261
  6.9 0.0 collective-permute-done.history_ref
  6.9 0.3 early.1
  7.2 3.5 %collective-permute-start.3 = (bf16[96,512]{1,0:T(8,128)(2,1)S(1)}, bf16[96,512]{1,0:T(8,128)(2,1)S(1)}, u32[]{:S(2)}, u32[]{:S(2)}) collective-permute-start(bf16[96,512]{1,0:T(8,128)(2,1)S(1)} %bitcast.20), channel_id=1, source_target_pairs={{0,8},{4,12},{8,0},{12,4},{1,9},{5,13},{9,1},{13,5},{2,10},{6,14},... | collective-permute-start | bytes 294920 | tf_op jit(solution)/shard_map/ppermute | solution.py:30
  10.7 1.3 %collective-permute-start.1 = (bf16[96,512]{1,0:T(8,128)(2,1)S(1)}, bf16[96,512]{1,0:T(8,128)(2,1)S(1)}, u32[]{:S(2)}, u32[]{:S(2)}) collective-permute-start(bf16[96,512]{1,0:T(8,128)(2,1)S(1)} %bitcast.21), channel_id=1, source_target_pairs={{0,12},{4,8},{8,4},{12,0},{1,13},{5,9},{9,5},{13,1},{2,14},{6,10},... | collective-permute-start | bytes 294920 | tf_op jit(solution)/shard_map/ppermute | solution.py:30
  12.0 2.8 %collective-permute-start.7 = (bf16[96,512]{1,0:T(8,128)(2,1)S(1)}, bf16[96,512]{1,0:T(8,128)(2,1)S(1)}, u32[]{:S(2)}, u32[]{:S(2)}) collective-permute-start(bf16[96,512]{1,0:T(8,128)(2,1)S(1)} %bitcast.18), channel_id=1, source_target_pairs={{0,6},{1,7},{2,4},{3,5},{4,2},{5,3},{6,0},{7,1},{8,14},{9,15},{10,... | collective-permute-start | bytes 294920 | tf_op jit(solution)/shard_map/ppermute | solution.py:364
  14.9 1.8 %collective-permute-start.6 = (bf16[96,512]{1,0:T(8,128)(2,1)S(1)}, bf16[96,512]{1,0:T(8,128)(2,1)S(1)}, u32[]{:S(2)}, u32[]{:S(2)}) collective-permute-start(bf16[96,512]{1,0:T(8,128)(2,1)S(1)} %bitcast.19), channel_id=1, source_target_pairs={{0,4},{4,0},{8,12},{12,8},{1,5},{5,1},{9,13},{13,9},{2,6},{6,2},{1... | collective-permute-start | bytes 294920 | tf_op jit(solution)/shard_map/ppermute | solution.py:30
  16.7 0.0 collective-permute-start.5
  16.7 0.0 collective-permute-done.3.refs_0_
  16.7 2.4 %collective-permute-start.4 = (bf16[96,512]{1,0:T(8,128)(2,1)S(1)}, bf16[96,512]{1,0:T(8,128)(2,1)S(1)}, u32[]{:S(2)}, u32[]{:S(2)}) collective-permute-start(bf16[96,512]{1,0:T(8,128)(2,1)S(1)} %collective-permute-done.3.refs_0_), channel_id=1, source_target_pairs={{0,2},{1,3},{2,0},{3,1},{4,6},{5,7},{6,4},{7,5},{8,10},{9,11},{10,... | collective-permute-start | bytes 294920 | tf_op jit(solution)/shard_map/ppermute | solution.py:30
  19.1 0.4 %choice.7.choice_ref = bf16[512,2048]{1,0:T(8,128)(2,1)S(1)} custom-call(s32[1,2048]{1,0:T(1,128)S(1)} %bitcast.13), custom_call_target="tpu_custom_call" | custom-call | tf_op jit(solution)/shard_map/choice/pallas_call | solution.py:261
  19.4 0.4 %choice.6.choice_ref = bf16[512,2048]{1,0:T(8,128)(2,1)S(1)} custom-call(s32[1,2048]{1,0:T(1,128)S(1)} %bitcast.14), custom_call_target="tpu_custom_call" | custom-call | tf_op jit(solution)/shard_map/choice/pallas_call | solution.py:261
  19.8 0.4 %choice.5.choice_ref = bf16[512,2048]{1,0:T(8,128)(2,1)S(1)} custom-call(s32[1,2048]{1,0:T(1,128)S(1)} %bitcast.15), custom_call_target="tpu_custom_call" | custom-call | tf_op jit(solution)/shard_map/choice/pallas_call | solution.py:261
  20.2 0.4 %choice.4.choice_ref = bf16[512,2048]{1,0:T(8,128)(2,1)S(1)} custom-call(s32[1,2048]{1,0:T(1,128)S(1)} %bitcast.16), custom_call_target="tpu_custom_call" | custom-call | tf_op jit(solution)/shard_map/choice/pallas_call | solution.py:261
  20.5 0.0 collective-permute-done.1.refs_0_
  20.6 0.8 %collective-permute-start.2 = (bf16[96,512]{1,0:T(8,128)(2,1)S(1)}, bf16[96,512]{1,0:T(8,128)(2,1)S(1)}, u32[]{:S(2)}, u32[]{:S(2)}) collective-permute-start(bf16[96,512]{1,0:T(8,128)(2,1)S(1)} %collective-permute-done.1.refs_0_), channel_id=1, source_target_pairs={{0,2},{1,3},{2,0},{3,1},{4,6},{5,7},{6,4},{7,5},{8,10},{9,11},{10,... | collective-permute-start | bytes 294920 | tf_op jit(solution)/shard_map/ppermute | solution.py:30
  21.3 0.0 collective-permute-done.7.refs_1_
  21.3 0.2 collective-permute-done.6.refs_0_
  21.6 0.6 %order.4.refs_2_ = bf16[96,4096]{1,0:T(8,128)(2,1)S(1)} custom-call(bf16[512,2048]{1,0:T(8,128)(2,1)S(1)} %choice.7.choice_ref, bf16[96,512]{1,0:T(8,128)(2,1)S(1)} %collective-permute-done.6.refs_0_, bf16[96,512]{1,0:T(8,128)(2,1)S(1)} %collective-permute-done.7.refs_1_), custom_call_target="tpu_custom_call" | custom-call | flops 402653184 | tf_op jit(solution)/shard_map/order/pallas_call | solution.py:261
  22.1 0.0 collective-permute-done.5.refs_1_
  22.2 0.6 %order.5.refs_2_ = bf16[96,4096]{1,0:T(8,128)(2,1)S(1)} custom-call(bf16[512,2048]{1,0:T(8,128)(2,1)S(1)} %choice.6.choice_ref, bf16[96,512]{1,0:T(8,128)(2,1)S(1)} %bitcast.12, bf16[96,512]{1,0:T(8,128)(2,1)S(1)} %collective-permute-done.5.refs_1_, bf16[96,4096]{1,0:T(8,128)(2,1)S(1)} %order.4.refs_2_), custom_call_target="tpu_custom_call", output_to_operand_aliasing={{}: (3, {})} | custom-call | flops 402653184 | tf_op jit(solution)/shard_map/order/pallas_call | solution.py:261
  22.8 0.4 %collective-permute-done.4.refs_1_ = bf16[96,512]{1,0:T(8,128)(2,1)S(1)} collective-permute-done((bf16[96,512]{1,0:T(8,128)(2,1)S(1)}, bf16[96,512]{1,0:T(8,128)(2,1)S(1)}, u32[]{:S(2)}, u32[]{:S(2)}) %collective-permute-start.4) | collective-permute-done | bytes 98336 | tf_op jit(solution)/shard_map/ppermute | solution.py:30
  23.1 0.6 %order.6.refs_2_ = bf16[96,4096]{1,0:T(8,128)(2,1)S(1)} custom-call(bf16[512,2048]{1,0:T(8,128)(2,1)S(1)} %choice.5.choice_ref, bf16[96,512]{1,0:T(8,128)(2,1)S(1)} %collective-permute-done.3.refs_0_, bf16[96,512]{1,0:T(8,128)(2,1)S(1)} %collective-permute-done.4.refs_1_, bf16[96,4096]{1,0:T(8,128)(2,1)S(1)} %order.5.refs_2_), custom_call_target="tpu_custom_call", output_to_operand_aliasing={{}: (3, {})} | custom-call | flops 402653184 | tf_op jit(solution)/shard_map/order/pallas_call | solution.py:261
  23.7 1.9 %collective-permute-done.2.refs_1_ = bf16[96,512]{1,0:T(8,128)(2,1)S(1)} collective-permute-done((bf16[96,512]{1,0:T(8,128)(2,1)S(1)}, bf16[96,512]{1,0:T(8,128)(2,1)S(1)}, u32[]{:S(2)}, u32[]{:S(2)}) %collective-permute-start.2) | collective-permute-done | bytes 98336 | tf_op jit(solution)/shard_map/ppermute | solution.py:30
  25.7 0.6 %order.7.refs_0_ = bf16[96,4096]{1,0:T(8,128)(2,1)S(1)} custom-call(bf16[512,2048]{1,0:T(8,128)(2,1)S(1)} %choice.4.choice_ref, bf16[96,512]{1,0:T(8,128)(2,1)S(1)} %collective-permute-done.1.refs_0_, bf16[96,512]{1,0:T(8,128)(2,1)S(1)} %collective-permute-done.2.refs_1_, bf16[96,4096]{1,0:T(8,128)(2,1)S(1)} %order.6.refs_2_), custom_call_target="tpu_custom_call", output_to_operand_aliasing={{}: (3, {})} | custom-call | flops 402653184 | tf_op jit(solution)/shard_map/order/pallas_call | solution.py:261
  26.3 0.1 collective-permute-start.8
  26.4 2.3 %collective-permute-done.8.refs_1_ = bf16[96,4096]{1,0:T(8,128)(2,1)S(1)} collective-permute-done((bf16[96,4096]{1,0:T(8,128)(2,1)S(1)}, bf16[96,4096]{1,0:T(8,128)(2,1)S(1)}, u32[]{:S(2)}, u32[]{:S(2)}) %collective-permute-start.8) | collective-permute-done | bytes 786464 | tf_op jit(solution)/shard_map/ppermute | solution.py:30
  28.7 3.9 %gram.1 = (bf16[48,4096]{1,0:T(8,128)(2,1)}, bf16[1024,4096]{1,0:T(8,128)(2,1)}) custom-call(bf16[96,4096]{1,0:T(8,128)(2,1)S(1)} %order.7.refs_0_, bf16[96,4096]{1,0:T(8,128)(2,1)S(1)} %collective-permute-done.8.refs_1_), custom_call_target="tpu_custom_call" | custom-call | bytes 12582912 | tf_op jit(solution)/shard_map/gram/pallas_call | solution.py:261
  (6 shorter events, 0.0 us)
Async XLA Ops:
  0.6 1.4 %copy-start = (bf16[512,2,1,768]{3,1,2,0:T(2,128)(2,1)S(1)}, bf16[512,2,1,768]{3,1,2,0:T(2,128)(2,1)}, u32[]{:S(2)}) copy-start(bf16[512,2,1,768]{3,1,2,0:T(2,128)(2,1)} %param.3) | copy-start | bytes 4718596
  2.0 3.0 %copy-start.1 = (bf16[512,2,1,768]{3,1,2,0:T(2,128)(2,1)S(1)}, bf16[512,2,1,768]{3,1,2,0:T(2,128)(2,1)}, u32[]{:S(2)}) copy-start(bf16[512,2,1,768]{3,1,2,0:T(2,128)(2,1)} %param.3) | copy-start | bytes 4718596
  2.0 4.9 %copy-start.3 = (bf16[512,2,1,48]{0,3,2,1:T(8,128)(2,1)S(1)}, bf16[512,2,1,48]{0,3,2,1:T(8,128)(2,1)}, u32[]{:S(2)}) copy-start(bf16[512,2,1,48]{0,3,2,1:T(8,128)(2,1)} %param.4) | copy-start | bytes 294916
  2.0 17.0 %copy-start.2 = (s32[2048]{0:T(1024)S(1)}, s32[2048]{0:T(1024)}, u32[]{:S(2)}) copy-start(s32[2048]{0:T(1024)} %param.5) | copy-start | bytes 24580
  2.5 4.4 %collective-permute-start = (f32[32,512]{1,0:T(8,128)S(1)}, f32[32,512]{1,0:T(8,128)S(1)}, u32[]{:S(2)}, u32[]{:S(2)}) collective-permute-start(f32[32,512]{1,0:T(8,128)S(1)} %history.1), channel_id=1, source_target_pairs={{0,1},{1,2},{2,3},{4,5},{5,6},{6,7},{8,9},{9,10},{10,11},{12,13},{... | collective-permute-start | bytes 196616 | tf_op jit(solution)/shard_map/ppermute | solution.py:25
  7.2 9.5 %collective-permute-start.3 = (bf16[96,512]{1,0:T(8,128)(2,1)S(1)}, bf16[96,512]{1,0:T(8,128)(2,1)S(1)}, u32[]{:S(2)}, u32[]{:S(2)}) collective-permute-start(bf16[96,512]{1,0:T(8,128)(2,1)S(1)} %bitcast.20), channel_id=1, source_target_pairs={{0,8},{4,12},{8,0},{12,4},{1,9},{5,13},{9,1},{13,5},{2,10},{6,14},... | collective-permute-start | bytes 294920 | tf_op jit(solution)/shard_map/ppermute | solution.py:30
  10.7 9.9 %collective-permute-start.1 = (bf16[96,512]{1,0:T(8,128)(2,1)S(1)}, bf16[96,512]{1,0:T(8,128)(2,1)S(1)}, u32[]{:S(2)}, u32[]{:S(2)}) collective-permute-start(bf16[96,512]{1,0:T(8,128)(2,1)S(1)} %bitcast.21), channel_id=1, source_target_pairs={{0,12},{4,8},{8,4},{12,0},{1,13},{5,9},{9,5},{13,1},{2,14},{6,10},... | collective-permute-start | bytes 294920 | tf_op jit(solution)/shard_map/ppermute | solution.py:30
  12.0 9.3 %collective-permute-start.7 = (bf16[96,512]{1,0:T(8,128)(2,1)S(1)}, bf16[96,512]{1,0:T(8,128)(2,1)S(1)}, u32[]{:S(2)}, u32[]{:S(2)}) collective-permute-start(bf16[96,512]{1,0:T(8,128)(2,1)S(1)} %bitcast.18), channel_id=1, source_target_pairs={{0,6},{1,7},{2,4},{3,5},{4,2},{5,3},{6,0},{7,1},{8,14},{9,15},{10,... | collective-permute-start | bytes 294920 | tf_op jit(solution)/shard_map/ppermute | solution.py:364
  14.9 6.7 %collective-permute-start.6 = (bf16[96,512]{1,0:T(8,128)(2,1)S(1)}, bf16[96,512]{1,0:T(8,128)(2,1)S(1)}, u32[]{:S(2)}, u32[]{:S(2)}) collective-permute-start(bf16[96,512]{1,0:T(8,128)(2,1)S(1)} %bitcast.19), channel_id=1, source_target_pairs={{0,4},{4,0},{8,12},{12,8},{1,5},{5,1},{9,13},{13,9},{2,6},{6,2},{1... | collective-permute-start | bytes 294920 | tf_op jit(solution)/shard_map/ppermute | solution.py:30
  16.7 5.5 %collective-permute-start.5 = (bf16[96,512]{1,0:T(8,128)(2,1)S(1)}, bf16[96,512]{1,0:T(8,128)(2,1)S(1)}, u32[]{:S(2)}, u32[]{:S(2)}) collective-permute-start(bf16[96,512]{1,0:T(8,128)(2,1)S(1)} %bitcast.11), channel_id=1, source_target_pairs={{0,2},{1,3},{2,0},{3,1},{4,6},{5,7},{6,4},{7,5},{8,10},{9,11},{10,... | collective-permute-start | bytes 294920 | tf_op jit(solution)/shard_map/ppermute | solution.py:30
  16.7 6.4 %collective-permute-start.4 = (bf16[96,512]{1,0:T(8,128)(2,1)S(1)}, bf16[96,512]{1,0:T(8,128)(2,1)S(1)}, u32[]{:S(2)}, u32[]{:S(2)}) collective-permute-start(bf16[96,512]{1,0:T(8,128)(2,1)S(1)} %collective-permute-done.3.refs_0_), channel_id=1, source_target_pairs={{0,2},{1,3},{2,0},{3,1},{4,6},{5,7},{6,4},{7,5},{8,10},{9,11},{10,... | collective-permute-start | bytes 294920 | tf_op jit(solution)/shard_map/ppermute | solution.py:30
  20.6 5.1 %collective-permute-start.2 = (bf16[96,512]{1,0:T(8,128)(2,1)S(1)}, bf16[96,512]{1,0:T(8,128)(2,1)S(1)}, u32[]{:S(2)}, u32[]{:S(2)}) collective-permute-start(bf16[96,512]{1,0:T(8,128)(2,1)S(1)} %collective-permute-done.1.refs_0_), channel_id=1, source_target_pairs={{0,2},{1,3},{2,0},{3,1},{4,6},{5,7},{6,4},{7,5},{8,10},{9,11},{10,... | collective-permute-start | bytes 294920 | tf_op jit(solution)/shard_map/ppermute | solution.py:30
  26.3 2.4 %collective-permute-start.8 = (bf16[96,4096]{1,0:T(8,128)(2,1)S(1)}, bf16[96,4096]{1,0:T(8,128)(2,1)S(1)}, u32[]{:S(2)}, u32[]{:S(2)}) collective-permute-start(bf16[96,4096]{1,0:T(8,128)(2,1)S(1)} %order.7.refs_0_), channel_id=1, source_target_pairs={{0,1},{1,0},{2,3},{3,2},{4,5},{5,4},{6,7},{7,6},{8,9},{9,8},{10,11... | collective-permute-start | bytes 2359304 | tf_op jit(solution)/shard_map/ppermute | solution.py:30

commit v4 on v3

--- a/solution.py
+++ b/solution.py
@@ -239,11 +239,11 @@
     for part in parts:
         ordered[row : row + part.shape[0], :] = part[...]
         row += part.shape[0]
-    place = pl.multiple_of(lax.axis_index("tblk") * width, width)
-    tile[...] = ordered[:, pl.ds(place, width)].T
-    chunk = width // 8
-    for at in range(8):
+    chunk = max(PAD, width // 8)
+    for at in range(width // chunk):
         rows = slice(at * chunk, (at + 1) * chunk)
+        place = pl.multiple_of(lax.axis_index("tblk") * width + at * chunk, chunk)
+        tile[rows, :] = ordered[:, pl.ds(place, chunk)].T
         gram = jnp.dot(tile[rows, :], ordered[...], preferred_element_type=jnp.float32)
         result[rows, :] = (gram * (1.0 / ordered.shape[0])).astype(jnp.bfloat16)
         copy = pltpu.make_async_copy(

time: 32.8 us -> 32.8 us (level)
  no operation moved by 1% of the time
where the time goes in v4:
time: 32.8 us; the launch traced here: 32.6 us
  starting transfers between devices  15.2 us (46%)
  Pallas kernels  10.4 us (32%)
  waiting for transfers between devices  4.8 us (15%)
  local copies, waits for them, and re-layouts  1.41 us (4%)
  between operations  0.78 us (2%)
    pallas_call x12, Pallas kernels, call(): pl.pallas_call(kernel, in_specs=spaces, out_specs=[outs] * len(shapes) if...  10.4 us
    ppermute x7, starting transfers between devices, swapped(): lax.ppermute(value, axis, [(source, source ^ distance) for source in rang...  9.87 us
    ppermute x7, waiting for transfers between devices, swapped(): lax.ppermute(value, axis, [(source, source ^ distance) for source in rang...  4.8 us
    ppermute x1, starting transfers between devices, local(): lax.ppermute(one, ('chan', 'tblk'), [(c * blocks + b, (c ^ 1) * blocks +...  2.83 us
    ppermute x1, starting transfers between devices, shifted(): lax.ppermute(value, axis, [(source, source + steps) for source in range(l...  2.49 us
    unnamed x8, local copies, waits for them, and re-layouts  1.41 us
  transfers between devices with their start and end apart: 9, of which 4 were waited for; matrix products, arithmetic and copies ran while one was open for 0% of the time, Pallas kernels for 16%

profile of v4, /device:TPU:0, one launch (start us, length us, event | category | flops | bytes accessed | tf_op | source)
XLA Modules:
  0.0 32.6 jit_solution(17939345339496083756)
XLA Ops:
  0.6 0.0 copy-start
  0.6 1.4 %copy-done = bf16[512,2,1,768]{3,1,2,0:T(2,128)(2,1)S(1)} copy-done((bf16[512,2,1,768]{3,1,2,0:T(2,128)(2,1)S(1)}, bf16[512,2,1,768]{3,1,2,0:T(2,128)(2,1)}, u32[]{:S(2)}) %copy-start) | copy-done | bytes 1572888
  2.0 0.5 %history.1 = f32[32,512]{1,0:T(8,128)S(1)} custom-call(bf16[512,1,2,768]{3,2,1,0:T(2,128)(2,1)S(1)} %bitcast.9), custom_call_target="tpu_custom_call" | custom-call | bytes 2097152 | tf_op jit(solution)/shard_map/history/pallas_call | solution.py:261
  2.5 2.5 %collective-permute-start = (f32[32,512]{1,0:T(8,128)S(1)}, f32[32,512]{1,0:T(8,128)S(1)}, u32[]{:S(2)}, u32[]{:S(2)}) collective-permute-start(f32[32,512]{1,0:T(8,128)S(1)} %history.1), channel_id=1, source_target_pairs={{0,1},{1,2},{2,3},{4,5},{5,6},{6,7},{8,9},{9,10},{10,11},{12,13},{... | collective-permute-start | bytes 196616 | tf_op jit(solution)/shard_map/ppermute | solution.py:25
  5.0 1.9 %channelize.1 = (bf16[1,96,512]{2,1,0:T(8,128)(2,1)S(1)}, bf16[1,96,512]{2,1,0:T(8,128)(2,1)S(1)}, bf16[1,96,512]{2,1,0:T(8,128)(2,1)S(1)}, bf16[1,96,512]{2,1,0:T(8,128)(2,1)S(1)}, f32[32,512]{1,0:T(8,128)S(1)}) custom-call(bf16[512,1,2,768]{3,2,1,0:T(2,128)(2,1)S(1)} %bitcast.10), custom_call_target="tpu_custom_call" | custom-call | bytes 6291456 | tf_op jit(solution)/shard_map/channelize/pallas_call | solution.py:261
  6.9 0.0 collective-permute-done.history_ref
  6.9 0.3 early.1
  7.2 3.5 %collective-permute-start.3 = (bf16[96,512]{1,0:T(8,128)(2,1)S(1)}, bf16[96,512]{1,0:T(8,128)(2,1)S(1)}, u32[]{:S(2)}, u32[]{:S(2)}) collective-permute-start(bf16[96,512]{1,0:T(8,128)(2,1)S(1)} %bitcast.20), channel_id=1, source_target_pairs={{0,8},{4,12},{8,0},{12,4},{1,9},{5,13},{9,1},{13,5},{2,10},{6,14},... | collective-permute-start | bytes 294920 | tf_op jit(solution)/shard_map/ppermute | solution.py:30
  10.7 1.3 %collective-permute-start.1 = (bf16[96,512]{1,0:T(8,128)(2,1)S(1)}, bf16[96,512]{1,0:T(8,128)(2,1)S(1)}, u32[]{:S(2)}, u32[]{:S(2)}) collective-permute-start(bf16[96,512]{1,0:T(8,128)(2,1)S(1)} %bitcast.21), channel_id=1, source_target_pairs={{0,12},{4,8},{8,4},{12,0},{1,13},{5,9},{9,5},{13,1},{2,14},{6,10},... | collective-permute-start | bytes 294920 | tf_op jit(solution)/shard_map/ppermute | solution.py:30
  12.0 2.8 %collective-permute-start.7 = (bf16[96,512]{1,0:T(8,128)(2,1)S(1)}, bf16[96,512]{1,0:T(8,128)(2,1)S(1)}, u32[]{:S(2)}, u32[]{:S(2)}) collective-permute-start(bf16[96,512]{1,0:T(8,128)(2,1)S(1)} %bitcast.18), channel_id=1, source_target_pairs={{0,6},{1,7},{2,4},{3,5},{4,2},{5,3},{6,0},{7,1},{8,14},{9,15},{10,... | collective-permute-start | bytes 294920 | tf_op jit(solution)/shard_map/ppermute | solution.py:364
  14.9 1.8 %collective-permute-start.6 = (bf16[96,512]{1,0:T(8,128)(2,1)S(1)}, bf16[96,512]{1,0:T(8,128)(2,1)S(1)}, u32[]{:S(2)}, u32[]{:S(2)}) collective-permute-start(bf16[96,512]{1,0:T(8,128)(2,1)S(1)} %bitcast.19), channel_id=1, source_target_pairs={{0,4},{4,0},{8,12},{12,8},{1,5},{5,1},{9,13},{13,9},{2,6},{6,2},{1... | collective-permute-start | bytes 294920 | tf_op jit(solution)/shard_map/ppermute | solution.py:30
  16.7 0.0 collective-permute-start.5
  16.7 0.0 collective-permute-done.3.refs_0_
  16.7 2.4 %collective-permute-start.4 = (bf16[96,512]{1,0:T(8,128)(2,1)S(1)}, bf16[96,512]{1,0:T(8,128)(2,1)S(1)}, u32[]{:S(2)}, u32[]{:S(2)}) collective-permute-start(bf16[96,512]{1,0:T(8,128)(2,1)S(1)} %collective-permute-done.3.refs_0_), channel_id=1, source_target_pairs={{0,2},{1,3},{2,0},{3,1},{4,6},{5,7},{6,4},{7,5},{8,10},{9,11},{10,... | collective-permute-start | bytes 294920 | tf_op jit(solution)/shard_map/ppermute | solution.py:30
  19.1 0.4 %choice.7.choice_ref = bf16[512,2048]{1,0:T(8,128)(2,1)S(1)} custom-call(s32[1,2048]{1,0:T(1,128)S(1)} %bitcast.13), custom_call_target="tpu_custom_call" | custom-call | tf_op jit(solution)/shard_map/choice/pallas_call | solution.py:261
  19.4 0.4 %choice.6.choice_ref = bf16[512,2048]{1,0:T(8,128)(2,1)S(1)} custom-call(s32[1,2048]{1,0:T(1,128)S(1)} %bitcast.14), custom_call_target="tpu_custom_call" | custom-call | tf_op jit(solution)/shard_map/choice/pallas_call | solution.py:261
  19.8 0.4 %choice.5.choice_ref = bf16[512,2048]{1,0:T(8,128)(2,1)S(1)} custom-call(s32[1,2048]{1,0:T(1,128)S(1)} %bitcast.15), custom_call_target="tpu_custom_call" | custom-call | tf_op jit(solution)/shard_map/choice/pallas_call | solution.py:261
  20.2 0.4 %choice.4.choice_ref = bf16[512,2048]{1,0:T(8,128)(2,1)S(1)} custom-call(s32[1,2048]{1,0:T(1,128)S(1)} %bitcast.16), custom_call_target="tpu_custom_call" | custom-call | tf_op jit(solution)/shard_map/choice/pallas_call | solution.py:261
  20.5 0.0 collective-permute-done.1.refs_0_
  20.6 0.8 %collective-permute-start.2 = (bf16[96,512]{1,0:T(8,128)(2,1)S(1)}, bf16[96,512]{1,0:T(8,128)(2,1)S(1)}, u32[]{:S(2)}, u32[]{:S(2)}) collective-permute-start(bf16[96,512]{1,0:T(8,128)(2,1)S(1)} %collective-permute-done.1.refs_0_), channel_id=1, source_target_pairs={{0,2},{1,3},{2,0},{3,1},{4,6},{5,7},{6,4},{7,5},{8,10},{9,11},{10,... | collective-permute-start | bytes 294920 | tf_op jit(solution)/shard_map/ppermute | solution.py:30
  21.3 0.0 collective-permute-done.7.refs_1_
  21.3 0.2 collective-permute-done.6.refs_0_
  21.6 0.6 %order.4.refs_2_ = bf16[96,4096]{1,0:T(8,128)(2,1)S(1)} custom-call(bf16[512,2048]{1,0:T(8,128)(2,1)S(1)} %choice.7.choice_ref, bf16[96,512]{1,0:T(8,128)(2,1)S(1)} %collective-permute-done.6.refs_0_, bf16[96,512]{1,0:T(8,128)(2,1)S(1)} %collective-permute-done.7.refs_1_), custom_call_target="tpu_custom_call" | custom-call | flops 402653184 | tf_op jit(solution)/shard_map/order/pallas_call | solution.py:261
  22.1 0.0 collective-permute-done.5.refs_1_
  22.2 0.6 %order.5.refs_2_ = bf16[96,4096]{1,0:T(8,128)(2,1)S(1)} custom-call(bf16[512,2048]{1,0:T(8,128)(2,1)S(1)} %choice.6.choice_ref, bf16[96,512]{1,0:T(8,128)(2,1)S(1)} %bitcast.12, bf16[96,512]{1,0:T(8,128)(2,1)S(1)} %collective-permute-done.5.refs_1_, bf16[96,4096]{1,0:T(8,128)(2,1)S(1)} %order.4.refs_2_), custom_call_target="tpu_custom_call", output_to_operand_aliasing={{}: (3, {})} | custom-call | flops 402653184 | tf_op jit(solution)/shard_map/order/pallas_call | solution.py:261
  22.8 0.4 %collective-permute-done.4.refs_1_ = bf16[96,512]{1,0:T(8,128)(2,1)S(1)} collective-permute-done((bf16[96,512]{1,0:T(8,128)(2,1)S(1)}, bf16[96,512]{1,0:T(8,128)(2,1)S(1)}, u32[]{:S(2)}, u32[]{:S(2)}) %collective-permute-start.4) | collective-permute-done | bytes 98336 | tf_op jit(solution)/shard_map/ppermute | solution.py:30
  23.1 0.6 %order.6.refs_2_ = bf16[96,4096]{1,0:T(8,128)(2,1)S(1)} custom-call(bf16[512,2048]{1,0:T(8,128)(2,1)S(1)} %choice.5.choice_ref, bf16[96,512]{1,0:T(8,128)(2,1)S(1)} %collective-permute-done.3.refs_0_, bf16[96,512]{1,0:T(8,128)(2,1)S(1)} %collective-permute-done.4.refs_1_, bf16[96,4096]{1,0:T(8,128)(2,1)S(1)} %order.5.refs_2_), custom_call_target="tpu_custom_call", output_to_operand_aliasing={{}: (3, {})} | custom-call | flops 402653184 | tf_op jit(solution)/shard_map/order/pallas_call | solution.py:261
  23.7 1.9 %collective-permute-done.2.refs_1_ = bf16[96,512]{1,0:T(8,128)(2,1)S(1)} collective-permute-done((bf16[96,512]{1,0:T(8,128)(2,1)S(1)}, bf16[96,512]{1,0:T(8,128)(2,1)S(1)}, u32[]{:S(2)}, u32[]{:S(2)}) %collective-permute-start.2) | collective-permute-done | bytes 98336 | tf_op jit(solution)/shard_map/ppermute | solution.py:30
  25.7 0.6 %order.7.refs_0_ = bf16[96,4096]{1,0:T(8,128)(2,1)S(1)} custom-call(bf16[512,2048]{1,0:T(8,128)(2,1)S(1)} %choice.4.choice_ref, bf16[96,512]{1,0:T(8,128)(2,1)S(1)} %collective-permute-done.1.refs_0_, bf16[96,512]{1,0:T(8,128)(2,1)S(1)} %collective-permute-done.2.refs_1_, bf16[96,4096]{1,0:T(8,128)(2,1)S(1)} %order.6.refs_2_), custom_call_target="tpu_custom_call", output_to_operand_aliasing={{}: (3, {})} | custom-call | flops 402653184 | tf_op jit(solution)/shard_map/order/pallas_call | solution.py:261
  26.3 0.1 collective-permute-start.8
  26.4 2.3 %collective-permute-done.8.refs_1_ = bf16[96,4096]{1,0:T(8,128)(2,1)S(1)} collective-permute-done((bf16[96,4096]{1,0:T(8,128)(2,1)S(1)}, bf16[96,4096]{1,0:T(8,128)(2,1)S(1)}, u32[]{:S(2)}, u32[]{:S(2)}) %collective-permute-start.8) | collective-permute-done | bytes 786464 | tf_op jit(solution)/shard_map/ppermute | solution.py:30
  28.7 4.0 %gram.1 = (bf16[48,4096]{1,0:T(8,128)(2,1)}, bf16[1024,4096]{1,0:T(8,128)(2,1)}) custom-call(bf16[96,4096]{1,0:T(8,128)(2,1)S(1)} %order.7.refs_0_, bf16[96,4096]{1,0:T(8,128)(2,1)S(1)} %collective-permute-done.8.refs_1_), custom_call_target="tpu_custom_call" | custom-call | bytes 12582912 | tf_op jit(solution)/shard_map/gram/pallas_call | solution.py:261
  (6 shorter events, 0.0 us)
Async XLA Ops:
  0.6 1.4 %copy-start = (bf16[512,2,1,768]{3,1,2,0:T(2,128)(2,1)S(1)}, bf16[512,2,1,768]{3,1,2,0:T(2,128)(2,1)}, u32[]{:S(2)}) copy-start(bf16[512,2,1,768]{3,1,2,0:T(2,128)(2,1)} %param.3) | copy-start | bytes 4718596
  2.0 3.0 %copy-start.1 = (bf16[512,2,1,768]{3,1,2,0:T(2,128)(2,1)S(1)}, bf16[512,2,1,768]{3,1,2,0:T(2,128)(2,1)}, u32[]{:S(2)}) copy-start(bf16[512,2,1,768]{3,1,2,0:T(2,128)(2,1)} %param.3) | copy-start | bytes 4718596
  2.0 4.9 %copy-start.3 = (bf16[512,2,1,48]{0,3,2,1:T(8,128)(2,1)S(1)}, bf16[512,2,1,48]{0,3,2,1:T(8,128)(2,1)}, u32[]{:S(2)}) copy-start(bf16[512,2,1,48]{0,3,2,1:T(8,128)(2,1)} %param.4) | copy-start | bytes 294916
  2.0 17.0 %copy-start.2 = (s32[2048]{0:T(1024)S(1)}, s32[2048]{0:T(1024)}, u32[]{:S(2)}) copy-start(s32[2048]{0:T(1024)} %param.5) | copy-start | bytes 24580
  2.5 4.4 %collective-permute-start = (f32[32,512]{1,0:T(8,128)S(1)}, f32[32,512]{1,0:T(8,128)S(1)}, u32[]{:S(2)}, u32[]{:S(2)}) collective-permute-start(f32[32,512]{1,0:T(8,128)S(1)} %history.1), channel_id=1, source_target_pairs={{0,1},{1,2},{2,3},{4,5},{5,6},{6,7},{8,9},{9,10},{10,11},{12,13},{... | collective-permute-start | bytes 196616 | tf_op jit(solution)/shard_map/ppermute | solution.py:25
  7.2 9.5 %collective-permute-start.3 = (bf16[96,512]{1,0:T(8,128)(2,1)S(1)}, bf16[96,512]{1,0:T(8,128)(2,1)S(1)}, u32[]{:S(2)}, u32[]{:S(2)}) collective-permute-start(bf16[96,512]{1,0:T(8,128)(2,1)S(1)} %bitcast.20), channel_id=1, source_target_pairs={{0,8},{4,12},{8,0},{12,4},{1,9},{5,13},{9,1},{13,5},{2,10},{6,14},... | collective-permute-start | bytes 294920 | tf_op jit(solution)/shard_map/ppermute | solution.py:30
  10.7 9.9 %collective-permute-start.1 = (bf16[96,512]{1,0:T(8,128)(2,1)S(1)}, bf16[96,512]{1,0:T(8,128)(2,1)S(1)}, u32[]{:S(2)}, u32[]{:S(2)}) collective-permute-start(bf16[96,512]{1,0:T(8,128)(2,1)S(1)} %bitcast.21), channel_id=1, source_target_pairs={{0,12},{4,8},{8,4},{12,0},{1,13},{5,9},{9,5},{13,1},{2,14},{6,10},... | collective-permute-start | bytes 294920 | tf_op jit(solution)/shard_map/ppermute | solution.py:30
  12.0 9.3 %collective-permute-start.7 = (bf16[96,512]{1,0:T(8,128)(2,1)S(1)}, bf16[96,512]{1,0:T(8,128)(2,1)S(1)}, u32[]{:S(2)}, u32[]{:S(2)}) collective-permute-start(bf16[96,512]{1,0:T(8,128)(2,1)S(1)} %bitcast.18), channel_id=1, source_target_pairs={{0,6},{1,7},{2,4},{3,5},{4,2},{5,3},{6,0},{7,1},{8,14},{9,15},{10,... | collective-permute-start | bytes 294920 | tf_op jit(solution)/shard_map/ppermute | solution.py:364
  14.9 6.7 %collective-permute-start.6 = (bf16[96,512]{1,0:T(8,128)(2,1)S(1)}, bf16[96,512]{1,0:T(8,128)(2,1)S(1)}, u32[]{:S(2)}, u32[]{:S(2)}) collective-permute-start(bf16[96,512]{1,0:T(8,128)(2,1)S(1)} %bitcast.19), channel_id=1, source_target_pairs={{0,4},{4,0},{8,12},{12,8},{1,5},{5,1},{9,13},{13,9},{2,6},{6,2},{1... | collective-permute-start | bytes 294920 | tf_op jit(solution)/shard_map/ppermute | solution.py:30
  16.7 5.5 %collective-permute-start.5 = (bf16[96,512]{1,0:T(8,128)(2,1)S(1)}, bf16[96,512]{1,0:T(8,128)(2,1)S(1)}, u32[]{:S(2)}, u32[]{:S(2)}) collective-permute-start(bf16[96,512]{1,0:T(8,128)(2,1)S(1)} %bitcast.11), channel_id=1, source_target_pairs={{0,2},{1,3},{2,0},{3,1},{4,6},{5,7},{6,4},{7,5},{8,10},{9,11},{10,... | collective-permute-start | bytes 294920 | tf_op jit(solution)/shard_map/ppermute | solution.py:30
  16.7 6.4 %collective-permute-start.4 = (bf16[96,512]{1,0:T(8,128)(2,1)S(1)}, bf16[96,512]{1,0:T(8,128)(2,1)S(1)}, u32[]{:S(2)}, u32[]{:S(2)}) collective-permute-start(bf16[96,512]{1,0:T(8,128)(2,1)S(1)} %collective-permute-done.3.refs_0_), channel_id=1, source_target_pairs={{0,2},{1,3},{2,0},{3,1},{4,6},{5,7},{6,4},{7,5},{8,10},{9,11},{10,... | collective-permute-start | bytes 294920 | tf_op jit(solution)/shard_map/ppermute | solution.py:30
  20.6 5.1 %collective-permute-start.2 = (bf16[96,512]{1,0:T(8,128)(2,1)S(1)}, bf16[96,512]{1,0:T(8,128)(2,1)S(1)}, u32[]{:S(2)}, u32[]{:S(2)}) collective-permute-start(bf16[96,512]{1,0:T(8,128)(2,1)S(1)} %collective-permute-done.1.refs_0_), channel_id=1, source_target_pairs={{0,2},{1,3},{2,0},{3,1},{4,6},{5,7},{6,4},{7,5},{8,10},{9,11},{10,... | collective-permute-start | bytes 294920 | tf_op jit(solution)/shard_map/ppermute | solution.py:30
  26.3 2.4 %collective-permute-start.8 = (bf16[96,4096]{1,0:T(8,128)(2,1)S(1)}, bf16[96,4096]{1,0:T(8,128)(2,1)S(1)}, u32[]{:S(2)}, u32[]{:S(2)}) collective-permute-start(bf16[96,4096]{1,0:T(8,128)(2,1)S(1)} %order.7.refs_0_), channel_id=1, source_target_pairs={{0,1},{1,0},{2,3},{3,2},{4,5},{5,4},{6,7},{7,6},{8,9},{9,8},{10,11... | collective-permute-start | bytes 2359304 | tf_op jit(solution)/shard_map/ppermute | solution.py:30

commit v5 on v4

--- a/solution.py
+++ b/solution.py
@@ -186,13 +186,13 @@
     inputs = choice_ref.shape[1]
     stacked = [piece[at * rows : (at + 1) * rows, :] for piece, (_, at) in zip(pieces, places)]
     stacked = jnp.concatenate(stacked, axis=0)
-    for column in range(0, inputs, 256):
-        total = jnp.dot(stacked, choice_ref[:, column : column + 256], preferred_element_type=jnp.float32)
+    for column in range(0, inputs, 512):
+        total = jnp.dot(stacked, choice_ref[:, column : column + 512], preferred_element_type=jnp.float32)
         total = total.astype(jnp.bfloat16)
         for at, (place, _) in enumerate(places):
             for part in range(2):
                 value = total[at * rows + part * frames : at * rows + (part + 1) * frames]
-                to = (slice(place * frames, (place + 1) * frames), slice(part * inputs + column, part * inputs + column + 256))
+                to = (slice(place * frames, (place + 1) * frames), slice(part * inputs + column, part * inputs + column + 512))
                 new_ref[to] = value if fresh else old_ref[to] + value
 
 

time: 32.8 us -> 32.8 us (level)
  no operation moved by 1% of the time
where the time goes in v5:
time: 32.8 us; the launch traced here: 32.6 us
  starting transfers between devices  15.2 us (46%)
  Pallas kernels  10.4 us (32%)
  waiting for transfers between devices  4.8 us (15%)
  local copies, waits for them, and re-layouts  1.41 us (4%)
  between operations  0.78 us (2%)
    pallas_call x12, Pallas kernels, call(): pl.pallas_call(kernel, in_specs=spaces, out_specs=[outs] * len(shapes) if...  10.4 us
    ppermute x7, starting transfers between devices, swapped(): lax.ppermute(value, axis, [(source, source ^ distance) for source in rang...  9.87 us
    ppermute x7, waiting for transfers between devices, swapped(): lax.ppermute(value, axis, [(source, source ^ distance) for source in rang...  4.8 us
    ppermute x1, starting transfers between devices, local(): lax.ppermute(one, ('chan', 'tblk'), [(c * blocks + b, (c ^ 1) * blocks +...  2.83 us
    ppermute x1, starting transfers between devices, shifted(): lax.ppermute(value, axis, [(source, source + steps) for source in range(l...  2.49 us
    unnamed x8, local copies, waits for them, and re-layouts  1.41 us
  transfers between devices with their start and end apart: 9, of which 4 were waited for; matrix products, arithmetic and copies ran while one was open for 0% of the time, Pallas kernels for 16%

profile of v5, /device:TPU:0, one launch (start us, length us, event | category | flops | bytes accessed | tf_op | source)
XLA Modules:
  0.0 32.6 jit_solution(17939345339496083756)
XLA Ops:
  0.6 0.0 copy-start
  0.6 1.4 %copy-done = bf16[512,2,1,768]{3,1,2,0:T(2,128)(2,1)S(1)} copy-done((bf16[512,2,1,768]{3,1,2,0:T(2,128)(2,1)S(1)}, bf16[512,2,1,768]{3,1,2,0:T(2,128)(2,1)}, u32[]{:S(2)}) %copy-start) | copy-done | bytes 1572888
  2.0 0.5 %history.1 = f32[32,512]{1,0:T(8,128)S(1)} custom-call(bf16[512,1,2,768]{3,2,1,0:T(2,128)(2,1)S(1)} %bitcast.9), custom_call_target="tpu_custom_call" | custom-call | bytes 2097152 | tf_op jit(solution)/shard_map/history/pallas_call | solution.py:261
  2.5 2.5 %collective-permute-start = (f32[32,512]{1,0:T(8,128)S(1)}, f32[32,512]{1,0:T(8,128)S(1)}, u32[]{:S(2)}, u32[]{:S(2)}) collective-permute-start(f32[32,512]{1,0:T(8,128)S(1)} %history.1), channel_id=1, source_target_pairs={{0,1},{1,2},{2,3},{4,5},{5,6},{6,7},{8,9},{9,10},{10,11},{12,13},{... | collective-permute-start | bytes 196616 | tf_op jit(solution)/shard_map/ppermute | solution.py:25
  5.0 1.9 %channelize.1 = (bf16[1,96,512]{2,1,0:T(8,128)(2,1)S(1)}, bf16[1,96,512]{2,1,0:T(8,128)(2,1)S(1)}, bf16[1,96,512]{2,1,0:T(8,128)(2,1)S(1)}, bf16[1,96,512]{2,1,0:T(8,128)(2,1)S(1)}, f32[32,512]{1,0:T(8,128)S(1)}) custom-call(bf16[512,1,2,768]{3,2,1,0:T(2,128)(2,1)S(1)} %bitcast.10), custom_call_target="tpu_custom_call" | custom-call | bytes 6291456 | tf_op jit(solution)/shard_map/channelize/pallas_call | solution.py:261
  6.9 0.0 collective-permute-done.history_ref
  6.9 0.3 early.1
  7.2 3.5 %collective-permute-start.3 = (bf16[96,512]{1,0:T(8,128)(2,1)S(1)}, bf16[96,512]{1,0:T(8,128)(2,1)S(1)}, u32[]{:S(2)}, u32[]{:S(2)}) collective-permute-start(bf16[96,512]{1,0:T(8,128)(2,1)S(1)} %bitcast.20), channel_id=1, source_target_pairs={{0,8},{4,12},{8,0},{12,4},{1,9},{5,13},{9,1},{13,5},{2,10},{6,14},... | collective-permute-start | bytes 294920 | tf_op jit(solution)/shard_map/ppermute | solution.py:30
  10.7 1.3 %collective-permute-start.1 = (bf16[96,512]{1,0:T(8,128)(2,1)S(1)}, bf16[96,512]{1,0:T(8,128)(2,1)S(1)}, u32[]{:S(2)}, u32[]{:S(2)}) collective-permute-start(bf16[96,512]{1,0:T(8,128)(2,1)S(1)} %bitcast.21), channel_id=1, source_target_pairs={{0,12},{4,8},{8,4},{12,0},{1,13},{5,9},{9,5},{13,1},{2,14},{6,10},... | collective-permute-start | bytes 294920 | tf_op jit(solution)/shard_map/ppermute | solution.py:30
  12.0 2.8 %collective-permute-start.7 = (bf16[96,512]{1,0:T(8,128)(2,1)S(1)}, bf16[96,512]{1,0:T(8,128)(2,1)S(1)}, u32[]{:S(2)}, u32[]{:S(2)}) collective-permute-start(bf16[96,512]{1,0:T(8,128)(2,1)S(1)} %bitcast.18), channel_id=1, source_target_pairs={{0,6},{1,7},{2,4},{3,5},{4,2},{5,3},{6,0},{7,1},{8,14},{9,15},{10,... | collective-permute-start | bytes 294920 | tf_op jit(solution)/shard_map/ppermute | solution.py:364
  14.9 1.8 %collective-permute-start.6 = (bf16[96,512]{1,0:T(8,128)(2,1)S(1)}, bf16[96,512]{1,0:T(8,128)(2,1)S(1)}, u32[]{:S(2)}, u32[]{:S(2)}) collective-permute-start(bf16[96,512]{1,0:T(8,128)(2,1)S(1)} %bitcast.19), channel_id=1, source_target_pairs={{0,4},{4,0},{8,12},{12,8},{1,5},{5,1},{9,13},{13,9},{2,6},{6,2},{1... | collective-permute-start | bytes 294920 | tf_op jit(solution)/shard_map/ppermute | solution.py:30
  16.7 0.0 collective-permute-start.5
  16.7 0.0 collective-permute-done.3.refs_0_
  16.7 2.4 %collective-permute-start.4 = (bf16[96,512]{1,0:T(8,128)(2,1)S(1)}, bf16[96,512]{1,0:T(8,128)(2,1)S(1)}, u32[]{:S(2)}, u32[]{:S(2)}) collective-permute-start(bf16[96,512]{1,0:T(8,128)(2,1)S(1)} %collective-permute-done.3.refs_0_), channel_id=1, source_target_pairs={{0,2},{1,3},{2,0},{3,1},{4,6},{5,7},{6,4},{7,5},{8,10},{9,11},{10,... | collective-permute-start | bytes 294920 | tf_op jit(solution)/shard_map/ppermute | solution.py:30
  19.1 0.4 %choice.7.choice_ref = bf16[512,2048]{1,0:T(8,128)(2,1)S(1)} custom-call(s32[1,2048]{1,0:T(1,128)S(1)} %bitcast.13), custom_call_target="tpu_custom_call" | custom-call | tf_op jit(solution)/shard_map/choice/pallas_call | solution.py:261
  19.4 0.4 %choice.6.choice_ref = bf16[512,2048]{1,0:T(8,128)(2,1)S(1)} custom-call(s32[1,2048]{1,0:T(1,128)S(1)} %bitcast.14), custom_call_target="tpu_custom_call" | custom-call | tf_op jit(solution)/shard_map/choice/pallas_call | solution.py:261
  19.8 0.4 %choice.5.choice_ref = bf16[512,2048]{1,0:T(8,128)(2,1)S(1)} custom-call(s32[1,2048]{1,0:T(1,128)S(1)} %bitcast.15), custom_call_target="tpu_custom_call" | custom-call | tf_op jit(solution)/shard_map/choice/pallas_call | solution.py:261
  20.2 0.4 %choice.4.choice_ref = bf16[512,2048]{1,0:T(8,128)(2,1)S(1)} custom-call(s32[1,2048]{1,0:T(1,128)S(1)} %bitcast.16), custom_call_target="tpu_custom_call" | custom-call | tf_op jit(solution)/shard_map/choice/pallas_call | solution.py:261
  20.5 0.0 collective-permute-done.1.refs_0_
  20.6 0.8 %collective-permute-start.2 = (bf16[96,512]{1,0:T(8,128)(2,1)S(1)}, bf16[96,512]{1,0:T(8,128)(2,1)S(1)}, u32[]{:S(2)}, u32[]{:S(2)}) collective-permute-start(bf16[96,512]{1,0:T(8,128)(2,1)S(1)} %collective-permute-done.1.refs_0_), channel_id=1, source_target_pairs={{0,2},{1,3},{2,0},{3,1},{4,6},{5,7},{6,4},{7,5},{8,10},{9,11},{10,... | collective-permute-start | bytes 294920 | tf_op jit(solution)/shard_map/ppermute | solution.py:30
  21.3 0.0 collective-permute-done.7.refs_1_
  21.3 0.2 collective-permute-done.6.refs_0_
  21.6 0.6 %order.4.refs_2_ = bf16[96,4096]{1,0:T(8,128)(2,1)S(1)} custom-call(bf16[512,2048]{1,0:T(8,128)(2,1)S(1)} %choice.7.choice_ref, bf16[96,512]{1,0:T(8,128)(2,1)S(1)} %collective-permute-done.6.refs_0_, bf16[96,512]{1,0:T(8,128)(2,1)S(1)} %collective-permute-done.7.refs_1_), custom_call_target="tpu_custom_call" | custom-call | flops 402653184 | tf_op jit(solution)/shard_map/order/pallas_call | solution.py:261
  22.1 0.0 collective-permute-done.5.refs_1_
  22.2 0.6 %order.5.refs_2_ = bf16[96,4096]{1,0:T(8,128)(2,1)S(1)} custom-call(bf16[512,2048]{1,0:T(8,128)(2,1)S(1)} %choice.6.choice_ref, bf16[96,512]{1,0:T(8,128)(2,1)S(1)} %bitcast.12, bf16[96,512]{1,0:T(8,128)(2,1)S(1)} %collective-permute-done.5.refs_1_, bf16[96,4096]{1,0:T(8,128)(2,1)S(1)} %order.4.refs_2_), custom_call_target="tpu_custom_call", output_to_operand_aliasing={{}: (3, {})} | custom-call | flops 402653184 | tf_op jit(solution)/shard_map/order/pallas_call | solution.py:261
  22.8 0.4 %collective-permute-done.4.refs_1_ = bf16[96,512]{1,0:T(8,128)(2,1)S(1)} collective-permute-done((bf16[96,512]{1,0:T(8,128)(2,1)S(1)}, bf16[96,512]{1,0:T(8,128)(2,1)S(1)}, u32[]{:S(2)}, u32[]{:S(2)}) %collective-permute-start.4) | collective-permute-done | bytes 98336 | tf_op jit(solution)/shard_map/ppermute | solution.py:30
  23.1 0.6 %order.6.refs_2_ = bf16[96,4096]{1,0:T(8,128)(2,1)S(1)} custom-call(bf16[512,2048]{1,0:T(8,128)(2,1)S(1)} %choice.5.choice_ref, bf16[96,512]{1,0:T(8,128)(2,1)S(1)} %collective-permute-done.3.refs_0_, bf16[96,512]{1,0:T(8,128)(2,1)S(1)} %collective-permute-done.4.refs_1_, bf16[96,4096]{1,0:T(8,128)(2,1)S(1)} %order.5.refs_2_), custom_call_target="tpu_custom_call", output_to_operand_aliasing={{}: (3, {})} | custom-call | flops 402653184 | tf_op jit(solution)/shard_map/order/pallas_call | solution.py:261
  23.7 1.9 %collective-permute-done.2.refs_1_ = bf16[96,512]{1,0:T(8,128)(2,1)S(1)} collective-permute-done((bf16[96,512]{1,0:T(8,128)(2,1)S(1)}, bf16[96,512]{1,0:T(8,128)(2,1)S(1)}, u32[]{:S(2)}, u32[]{:S(2)}) %collective-permute-start.2) | collective-permute-done | bytes 98336 | tf_op jit(solution)/shard_map/ppermute | solution.py:30
  25.7 0.6 %order.7.refs_0_ = bf16[96,4096]{1,0:T(8,128)(2,1)S(1)} custom-call(bf16[512,2048]{1,0:T(8,128)(2,1)S(1)} %choice.4.choice_ref, bf16[96,512]{1,0:T(8,128)(2,1)S(1)} %collective-permute-done.1.refs_0_, bf16[96,512]{1,0:T(8,128)(2,1)S(1)} %collective-permute-done.2.refs_1_, bf16[96,4096]{1,0:T(8,128)(2,1)S(1)} %order.6.refs_2_), custom_call_target="tpu_custom_call", output_to_operand_aliasing={{}: (3, {})} | custom-call | flops 402653184 | tf_op jit(solution)/shard_map/order/pallas_call | solution.py:261
  26.3 0.1 collective-permute-start.8
  26.4 2.3 %collective-permute-done.8.refs_1_ = bf16[96,4096]{1,0:T(8,128)(2,1)S(1)} collective-permute-done((bf16[96,4096]{1,0:T(8,128)(2,1)S(1)}, bf16[96,4096]{1,0:T(8,128)(2,1)S(1)}, u32[]{:S(2)}, u32[]{:S(2)}) %collective-permute-start.8) | collective-permute-done | bytes 786464 | tf_op jit(solution)/shard_map/ppermute | solution.py:30
  28.7 4.0 %gram.1 = (bf16[48,4096]{1,0:T(8,128)(2,1)}, bf16[1024,4096]{1,0:T(8,128)(2,1)}) custom-call(bf16[96,4096]{1,0:T(8,128)(2,1)S(1)} %order.7.refs_0_, bf16[96,4096]{1,0:T(8,128)(2,1)S(1)} %collective-permute-done.8.refs_1_), custom_call_target="tpu_custom_call" | custom-call | bytes 12582912 | tf_op jit(solution)/shard_map/gram/pallas_call | solution.py:261
  (6 shorter events, 0.0 us)
Async XLA Ops:
  0.6 1.4 %copy-start = (bf16[512,2,1,768]{3,1,2,0:T(2,128)(2,1)S(1)}, bf16[512,2,1,768]{3,1,2,0:T(2,128)(2,1)}, u32[]{:S(2)}) copy-start(bf16[512,2,1,768]{3,1,2,0:T(2,128)(2,1)} %param.3) | copy-start | bytes 4718596
  2.0 3.0 %copy-start.1 = (bf16[512,2,1,768]{3,1,2,0:T(2,128)(2,1)S(1)}, bf16[512,2,1,768]{3,1,2,0:T(2,128)(2,1)}, u32[]{:S(2)}) copy-start(bf16[512,2,1,768]{3,1,2,0:T(2,128)(2,1)} %param.3) | copy-start | bytes 4718596
  2.0 4.9 %copy-start.3 = (bf16[512,2,1,48]{0,3,2,1:T(8,128)(2,1)S(1)}, bf16[512,2,1,48]{0,3,2,1:T(8,128)(2,1)}, u32[]{:S(2)}) copy-start(bf16[512,2,1,48]{0,3,2,1:T(8,128)(2,1)} %param.4) | copy-start | bytes 294916
  2.0 17.0 %copy-start.2 = (s32[2048]{0:T(1024)S(1)}, s32[2048]{0:T(1024)}, u32[]{:S(2)}) copy-start(s32[2048]{0:T(1024)} %param.5) | copy-start | bytes 24580
  2.5 4.4 %collective-permute-start = (f32[32,512]{1,0:T(8,128)S(1)}, f32[32,512]{1,0:T(8,128)S(1)}, u32[]{:S(2)}, u32[]{:S(2)}) collective-permute-start(f32[32,512]{1,0:T(8,128)S(1)} %history.1), channel_id=1, source_target_pairs={{0,1},{1,2},{2,3},{4,5},{5,6},{6,7},{8,9},{9,10},{10,11},{12,13},{... | collective-permute-start | bytes 196616 | tf_op jit(solution)/shard_map/ppermute | solution.py:25
  7.2 9.5 %collective-permute-start.3 = (bf16[96,512]{1,0:T(8,128)(2,1)S(1)}, bf16[96,512]{1,0:T(8,128)(2,1)S(1)}, u32[]{:S(2)}, u32[]{:S(2)}) collective-permute-start(bf16[96,512]{1,0:T(8,128)(2,1)S(1)} %bitcast.20), channel_id=1, source_target_pairs={{0,8},{4,12},{8,0},{12,4},{1,9},{5,13},{9,1},{13,5},{2,10},{6,14},... | collective-permute-start | bytes 294920 | tf_op jit(solution)/shard_map/ppermute | solution.py:30
  10.7 9.9 %collective-permute-start.1 = (bf16[96,512]{1,0:T(8,128)(2,1)S(1)}, bf16[96,512]{1,0:T(8,128)(2,1)S(1)}, u32[]{:S(2)}, u32[]{:S(2)}) collective-permute-start(bf16[96,512]{1,0:T(8,128)(2,1)S(1)} %bitcast.21), channel_id=1, source_target_pairs={{0,12},{4,8},{8,4},{12,0},{1,13},{5,9},{9,5},{13,1},{2,14},{6,10},... | collective-permute-start | bytes 294920 | tf_op jit(solution)/shard_map/ppermute | solution.py:30
  12.0 9.3 %collective-permute-start.7 = (bf16[96,512]{1,0:T(8,128)(2,1)S(1)}, bf16[96,512]{1,0:T(8,128)(2,1)S(1)}, u32[]{:S(2)}, u32[]{:S(2)}) collective-permute-start(bf16[96,512]{1,0:T(8,128)(2,1)S(1)} %bitcast.18), channel_id=1, source_target_pairs={{0,6},{1,7},{2,4},{3,5},{4,2},{5,3},{6,0},{7,1},{8,14},{9,15},{10,... | collective-permute-start | bytes 294920 | tf_op jit(solution)/shard_map/ppermute | solution.py:364
  14.9 6.7 %collective-permute-start.6 = (bf16[96,512]{1,0:T(8,128)(2,1)S(1)}, bf16[96,512]{1,0:T(8,128)(2,1)S(1)}, u32[]{:S(2)}, u32[]{:S(2)}) collective-permute-start(bf16[96,512]{1,0:T(8,128)(2,1)S(1)} %bitcast.19), channel_id=1, source_target_pairs={{0,4},{4,0},{8,12},{12,8},{1,5},{5,1},{9,13},{13,9},{2,6},{6,2},{1... | collective-permute-start | bytes 294920 | tf_op jit(solution)/shard_map/ppermute | solution.py:30
  16.7 5.5 %collective-permute-start.5 = (bf16[96,512]{1,0:T(8,128)(2,1)S(1)}, bf16[96,512]{1,0:T(8,128)(2,1)S(1)}, u32[]{:S(2)}, u32[]{:S(2)}) collective-permute-start(bf16[96,512]{1,0:T(8,128)(2,1)S(1)} %bitcast.11), channel_id=1, source_target_pairs={{0,2},{1,3},{2,0},{3,1},{4,6},{5,7},{6,4},{7,5},{8,10},{9,11},{10,... | collective-permute-start | bytes 294920 | tf_op jit(solution)/shard_map/ppermute | solution.py:30
  16.7 6.4 %collective-permute-start.4 = (bf16[96,512]{1,0:T(8,128)(2,1)S(1)}, bf16[96,512]{1,0:T(8,128)(2,1)S(1)}, u32[]{:S(2)}, u32[]{:S(2)}) collective-permute-start(bf16[96,512]{1,0:T(8,128)(2,1)S(1)} %collective-permute-done.3.refs_0_), channel_id=1, source_target_pairs={{0,2},{1,3},{2,0},{3,1},{4,6},{5,7},{6,4},{7,5},{8,10},{9,11},{10,... | collective-permute-start | bytes 294920 | tf_op jit(solution)/shard_map/ppermute | solution.py:30
  20.6 5.1 %collective-permute-start.2 = (bf16[96,512]{1,0:T(8,128)(2,1)S(1)}, bf16[96,512]{1,0:T(8,128)(2,1)S(1)}, u32[]{:S(2)}, u32[]{:S(2)}) collective-permute-start(bf16[96,512]{1,0:T(8,128)(2,1)S(1)} %collective-permute-done.1.refs_0_), channel_id=1, source_target_pairs={{0,2},{1,3},{2,0},{3,1},{4,6},{5,7},{6,4},{7,5},{8,10},{9,11},{10,... | collective-permute-start | bytes 294920 | tf_op jit(solution)/shard_map/ppermute | solution.py:30
  26.3 2.4 %collective-permute-start.8 = (bf16[96,4096]{1,0:T(8,128)(2,1)S(1)}, bf16[96,4096]{1,0:T(8,128)(2,1)S(1)}, u32[]{:S(2)}, u32[]{:S(2)}) collective-permute-start(bf16[96,4096]{1,0:T(8,128)(2,1)S(1)} %order.7.refs_0_), channel_id=1, source_target_pairs={{0,1},{1,0},{2,3},{3,2},{4,5},{5,4},{6,7},{7,6},{8,9},{9,8},{10,11... | collective-permute-start | bytes 2359304 | tf_op jit(solution)/shard_map/ppermute | solution.py:30
